TPU v7x, 32 devices: a whole 2x2x4 slice. The times are simulated.
32 devices in a mesh: dp: 4 (over y, x), row: 4 (over z), col: 2 (over core).
Axes of the slice: x: 2, y: 2, z: 4, core: 2. Of those that a mesh axis runs over, the one named last changes fastest.
Arguments:
- tokens: bfloat16 [1088, 8192], P('col', ('dp', 'row')), may hold values from -6 to 6
- ln1_gain: float32 [1088], P('col'), may hold values from 0.1 to 1.9
- ln1_bias: float32 [1088], P('col'), may hold values from -3 to 3
- qkv_weight: bfloat16 [1088, 3, 1088], P('col', None, 'row'), may hold values from -0.1875 to 0.1875
- qv_bias: bfloat16 [2, 1088], P(None, 'row'), may hold values from -3 to 3
- out_weight: bfloat16 [1088, 1088], P('row', 'col'), may hold values from -1.5 to 1.5
- out_bias: bfloat16 [1088], P('col'), may hold values from -3 to 3
- ln2_gain: float32 [1088], P('col'), may hold values from 0.1 to 1.9
- ln2_bias: float32 [1088], P('col'), may hold values from -3 to 3
- fc_weight: bfloat16 [1088, 4352], P('col', 'row'), may hold values from -0.1875 to 0.1875
- fc_bias: bfloat16 [4352], P('row'), may hold values from -3 to 3
- proj_weight: bfloat16 [1088, 4352], P('col', 'row'), may hold values from -0.09375 to 0.09375
- proj_bias: bfloat16 [1088], P('col'), may hold values from -3 to 3
- doc_lengths: int32 [8, 20], P(('dp', 'col')), may hold values from 0 to 1024, as said below
- cotangent: bfloat16 [1088, 8192], P('col', ('dp', 'row')), may hold values from -6 to 6
Outputs:
- output: bfloat16 [1088, 8192], P('col', ('dp', 'row'))
- input_grad: bfloat16 [1088, 8192], P('col', ('dp', 'row'))
- ln1_gain_grad: float32 [1088], P('col')
- ln1_bias_grad: float32 [1088], P('col')
- qkv_weight_grad: float32 [1088, 3, 1088], P('col', None, 'row')
- qv_bias_grad: float32 [2, 1088], P(None, 'row')
- out_weight_grad: float32 [1088, 1088], P('row', 'col')
- out_bias_grad: float32 [1088], P('col')
- ln2_gain_grad: float32 [1088], P('col')
- ln2_bias_grad: float32 [1088], P('col')
- fc_weight_grad: float32 [1088, 4352], P('col', 'row')
- fc_bias_grad: float32 [4352], P('row')
- proj_weight_grad: float32 [1088, 4352], P('col', 'row')
- proj_bias_grad: float32 [1088], P('col')
Inputs may be any that keep to these rules, and one draw needn't show every extreme that they name: `doc_lengths`: each row lists the lengths of one sequence's documents in order, zeros after the last; the positions after their sum (fewer than 64) are padding. In each run of 2 sequences starting at a multiple of 2, one holds a single document of all 1024 positions; in the others every document but the last has 64 to 512 tokens and the last at most 512.
All inputs are finite; a program needn't handle non-finite values.
Results may differ from a plain program's by a relative error of at most 0.012.
The roundings to bfloat16 on the way count: a program that leaves them out, or rounds other values in their place, can miss the bound.
Values may be sent and summed in bfloat16 or wider, within the bound.
A program may use at most 256 MiB of HBM per device.

v0:
```python
from functools import partial
import math

import jax
import jax.numpy as jnp
from jax import lax
from jax.sharding import PartitionSpec as P

HEAD_DIM = 64


epsilon = 1e-05
score_scale = 0.125
masked_fill = -1e30
block_limit = 512


def feature_sums(first_sum, second_sum):
    return lax.psum((first_sum, second_sum), "col")


def norm_forward(values, gain_vec, shift_vec):
    feature_count = values.shape[1] * lax.axis_size("col")
    total_sum, square_sum = feature_sums(jnp.sum(values, axis=1), jnp.sum(values * values, axis=1))
    center = total_sum / feature_count
    spread = square_sum / feature_count - center * center
    inv_std = lax.rsqrt(spread + epsilon)
    normal = (values - center[:, None]) * inv_std[:, None]
    return (normal, inv_std, normal * gain_vec + shift_vec)


def norm_backward(upstream, normal, inv_std, gain_vec):
    feature_count = upstream.shape[1] * lax.axis_size("col")
    scaled = upstream * gain_vec
    plain_sum, cross_sum = feature_sums(jnp.sum(scaled, axis=1), jnp.sum(scaled * normal, axis=1))
    return inv_std[:, None] * (
        scaled - plain_sum[:, None] / feature_count - normal * (cross_sum[:, None] / feature_count)
    )


def gather_rows(values):
    return lax.all_gather(values, "row", axis=0, tiled=True)


def gather_cols(values):
    return lax.all_gather(values, "col", axis=0, tiled=True)


def sum_over_rows(row_term, row_total):
    return lax.psum_scatter(
        row_term(jnp.int32(0), row_total * lax.axis_size("row")),
        "row",
        scatter_dimension=0,
        tiled=True,
    )


def sum_over_cols(row_term, row_total):
    return lax.psum_scatter(
        row_term(jnp.int32(0), row_total * lax.axis_size("col")),
        "col",
        scatter_dimension=0,
        tiled=True,
    )


def to_heads(values):
    return lax.all_to_all(values, "row", split_axis=0, concat_axis=2, tiled=True)


def to_tokens(values):
    return lax.all_to_all(values, "row", split_axis=2, concat_axis=0, tiled=True)


def product_term(full_rows, matrix):

    def row_term(first_row, row_count):
        return jnp.dot(full_rows, matrix, preferred_element_type=jnp.float32)

    return row_term


def product_term_back(full_rows, matrix):

    def row_term(first_row, row_count):
        return lax.dot_general(
            full_rows, matrix, (((1,), (1,)), ((), ())), preferred_element_type=jnp.float32
        )

    return row_term


def slice_term(full_rows):

    def row_term(first_row, row_count):
        return full_rows

    return row_term


def inner_rows(left_side, right_side):
    return lax.dot_general(
        left_side, right_side, (((0,), (0,)), ((), ())), preferred_element_type=jnp.float32
    )


def segments_of(lengths, places):
    doc_ends = jnp.cumsum(lengths)
    segment = jnp.sum(
        (doc_ends[None, :] <= places[:, None]).astype(jnp.int32), axis=1, dtype=jnp.int32
    )
    return (segment, places >= doc_ends[-1])


def allowed_pairs(query_place, query_segment, query_padding, key_place, key_segment):
    causal = key_place[None, :] <= query_place[:, None]
    same_doc = key_segment[None, :] == query_segment[:, None]
    itself = key_place[None, :] == query_place[:, None]
    return causal & same_doc & (jnp.logical_not(query_padding)[:, None] | itself)


def attention_parts(queries, keyvals, lengths, query_place):
    seq_total = keyvals.shape[0]
    key_block_size = math.gcd(seq_total, block_limit)
    block_count = seq_total // key_block_size
    key_place = jnp.arange(seq_total, dtype=jnp.int32)
    key_segment = segments_of(lengths, key_place)[0]
    query_segment, query_padding = segments_of(lengths, query_place)
    blocked = (
        keyvals.reshape((block_count, key_block_size) + keyvals.shape[1:]),
        key_place.reshape(block_count, key_block_size),
        key_segment.reshape(block_count, key_block_size),
    )

    def block_scores(key_rows, place_rows, segment_rows):
        raw_scores = (
            jnp.einsum("qhd,khd->hqk", queries, key_rows, preferred_element_type=jnp.float32)
            * score_scale
        )
        allowed = allowed_pairs(
            query_place, query_segment, query_padding, place_rows, segment_rows
        )[None]
        return (raw_scores, allowed)

    return (blocked, block_scores)


def attention_forward(queries, blocked, block_scores):
    query_count, head_count, head_width = queries.shape

    def max_step(running, inputs):
        best_score, mass_sum = running
        kv_block, place_rows, segment_rows = inputs
        raw_scores, allowed = block_scores(kv_block[:, 0], place_rows, segment_rows)
        masked = jnp.where(allowed, raw_scores, masked_fill)
        new_best = jnp.maximum(best_score, jnp.max(masked, axis=2))
        fresh = jnp.sum(jnp.where(allowed, jnp.exp(masked - new_best[:, :, None]), 0.0), axis=2)
        return ((new_best, mass_sum * jnp.exp(best_score - new_best) + fresh), None)

    start_best = jnp.full((head_count, query_count), masked_fill, jnp.float32)
    start_mass = jnp.zeros((head_count, query_count), jnp.float32)
    (best_score, mass_sum), unused = lax.scan(max_step, (start_best, start_mass), blocked)
    log_sum = best_score + jnp.log(mass_sum)

    def out_step(running, inputs):
        kv_block, place_rows, segment_rows = inputs
        raw_scores, allowed = block_scores(kv_block[:, 0], place_rows, segment_rows)
        probs_low = jnp.where(allowed, jnp.exp(raw_scores - log_sum[:, :, None]), 0.0).astype(
            jnp.bfloat16
        )
        return (
            running
            + jnp.einsum(
                "hqk,khd->qhd", probs_low, kv_block[:, 1], preferred_element_type=jnp.float32
            ),
            None,
        )

    attended, unused = lax.scan(
        out_step, jnp.zeros((query_count, head_count, head_width), jnp.float32), blocked
    )
    return (attended, log_sum)


def attention_backward(queries, blocked, block_scores, log_sum, grad_attended):
    query_count, head_count, head_width = queries.shape

    def probs_and_grads(inputs):
        kv_block, place_rows, segment_rows = inputs
        raw_scores, allowed = block_scores(kv_block[:, 0], place_rows, segment_rows)
        probs_f = jnp.where(allowed, jnp.exp(raw_scores - log_sum[:, :, None]), 0.0)
        grad_probs = jnp.einsum(
            "qhd,khd->hqk", grad_attended, kv_block[:, 1], preferred_element_type=jnp.float32
        )
        return (probs_f, grad_probs)

    def delta_step(running, inputs):
        probs_f, grad_probs = probs_and_grads(inputs)
        return (running + jnp.sum(probs_f * grad_probs, axis=2), None)

    delta_sum, unused = lax.scan(
        delta_step, jnp.zeros((head_count, query_count), jnp.float32), blocked
    )

    def grad_step(running, inputs):
        kv_block = inputs[0]
        probs_f, grad_probs = probs_and_grads(inputs)
        grad_scores = (probs_f * (grad_probs - delta_sum[:, :, None])).astype(jnp.bfloat16)
        running = running + jnp.einsum(
            "hqk,khd->qhd", grad_scores, kv_block[:, 0], preferred_element_type=jnp.float32
        )
        grad_keys = (
            jnp.einsum("hqk,qhd->khd", grad_scores, queries, preferred_element_type=jnp.float32)
            * score_scale
        )
        grad_values = jnp.einsum(
            "hqk,qhd->khd",
            probs_f.astype(jnp.bfloat16),
            grad_attended,
            preferred_element_type=jnp.float32,
        )
        return (running, jnp.stack([grad_keys, grad_values], axis=1))

    grad_queries, grad_keyvals = lax.scan(
        grad_step, jnp.zeros((query_count, head_count, head_width), jnp.float32), blocked
    )
    seq_total = grad_keyvals.shape[0] * grad_keyvals.shape[1]
    return (grad_queries * score_scale, grad_keyvals.reshape(seq_total, 2, head_count, head_width))


def body(
    tokens,
    ln1_gain,
    ln1_bias,
    qkv_weight,
    qv_bias,
    out_weight,
    out_bias,
    ln2_gain,
    ln2_bias,
    fc_weight,
    fc_bias,
    proj_weight,
    proj_bias,
    doc_lengths,
    cotangent,
):
    count_rows = lax.axis_size("row")
    count_cols = lax.axis_size("col")
    grid_rows = tokens.shape[1]
    col_width = tokens.shape[0]
    row_width = out_weight.shape[0]
    seq_rows = grid_rows * count_rows // count_cols
    query_rows = seq_rows // count_rows
    full_width = col_width * count_cols
    head_count = full_width // HEAD_DIM
    tokens_f = tokens.astype(jnp.float32).T
    normal1, inv_std1, shaped1 = norm_forward(tokens_f, ln1_gain, ln1_bias)
    qkv_flat = qkv_weight.reshape(col_width, 3 * row_width)
    gathered1 = gather_rows(shaped1.astype(jnp.bfloat16))
    mixed_qkv = sum_over_cols(product_term(gathered1, qkv_flat), seq_rows).reshape(
        seq_rows, 3, row_width
    )
    bias_three = jnp.stack([qv_bias[0], jnp.zeros_like(qv_bias[0]), qv_bias[1]])
    qkv_low = (mixed_qkv + bias_three).astype(jnp.bfloat16)
    local_qkv = to_heads(qkv_low).reshape(query_rows, 3, head_count, HEAD_DIM)
    queries = local_qkv[:, 0]
    keyvals = lax.all_gather(local_qkv[:, 1:], "row", axis=0, tiled=True)
    query_place = lax.axis_index("row") * query_rows + jnp.arange(query_rows, dtype=jnp.int32)
    blocked, block_scores = attention_parts(queries, keyvals, doc_lengths[0], query_place)
    attended_f, log_sum = attention_forward(queries, blocked, block_scores)
    attended_low = attended_f.reshape(query_rows, 1, full_width).astype(jnp.bfloat16)
    attended_grid = to_tokens(attended_low).reshape(seq_rows, row_width)
    gathered_att = gather_cols(attended_grid)
    branch = sum_over_rows(product_term(gathered_att, out_weight), grid_rows)
    hidden = tokens_f + (branch + out_bias)
    normal2, inv_std2, shaped2 = norm_forward(hidden, ln2_gain, ln2_bias)
    normed2 = shaped2.astype(jnp.bfloat16)
    gathered2 = gather_rows(normed2)
    pre_act = sum_over_cols(product_term(gathered2, fc_weight), seq_rows) + fc_bias
    active = jax.nn.gelu(pre_act, approximate=False).astype(jnp.bfloat16)
    gathered_act = gather_cols(active)
    projected = sum_over_rows(product_term_back(gathered_act, proj_weight), grid_rows)
    output = (hidden + projected + proj_bias).astype(jnp.bfloat16).T
    cotangent_rows = cotangent.T
    grad_out = cotangent_rows.astype(jnp.float32)
    unused, gelu_back = jax.vjp(partial(jax.nn.gelu, approximate=False), pre_act)
    grad_gathered = gather_rows(cotangent_rows)
    proj_weight_grad = inner_rows(grad_gathered, gathered_act)
    proj_bias_grad = jnp.sum(grad_gathered, axis=0, dtype=jnp.float32)
    grad_active = sum_over_cols(product_term(grad_gathered, proj_weight), seq_rows)
    grad_pre = gelu_back(grad_active)[0].astype(jnp.bfloat16)
    grad_pre_all = gather_cols(grad_pre)
    fc_weight_grad = inner_rows(gathered2, grad_pre_all)
    fc_bias_grad = jnp.sum(grad_pre_all, axis=0, dtype=jnp.float32)
    grad_normed2 = sum_over_rows(product_term_back(grad_pre_all, fc_weight), grid_rows)
    ln2_gain_part = jnp.sum(grad_normed2 * normal2, axis=0)
    ln2_bias_part = jnp.sum(grad_normed2, axis=0)
    grad_hidden = grad_out + norm_backward(grad_normed2, normal2, inv_std2, ln2_gain)
    branch_gathered = gather_rows(grad_hidden.astype(jnp.bfloat16))
    out_weight_grad = inner_rows(gathered_att, branch_gathered)
    out_bias_grad = jnp.sum(branch_gathered, axis=0, dtype=jnp.float32)
    grad_att_grid = sum_over_cols(product_term_back(branch_gathered, out_weight), seq_rows).astype(
        jnp.bfloat16
    )
    grad_attended = to_heads(grad_att_grid.reshape(seq_rows, 1, row_width)).reshape(
        query_rows, head_count, HEAD_DIM
    )
    grad_queries, grad_keyvals = attention_backward(
        queries, blocked, block_scores, log_sum, grad_attended
    )
    keyval_rows = sum_over_rows(slice_term(grad_keyvals), query_rows)
    grad_qkv_local = (
        jnp.concatenate([grad_queries[:, None], keyval_rows], axis=1)
        .astype(jnp.bfloat16)
        .reshape(query_rows, 3, full_width)
    )
    grad_qkv_grid = to_tokens(grad_qkv_local).reshape(seq_rows, 3 * row_width)
    qkv_gathered = gather_cols(grad_qkv_grid)
    qkv_weight_grad = inner_rows(gathered1, qkv_gathered).reshape(col_width, 3, row_width)
    qkv_bias_sums = jnp.sum(qkv_gathered, axis=0, dtype=jnp.float32).reshape(3, row_width)
    qv_bias_grad = jnp.stack([qkv_bias_sums[0], qkv_bias_sums[2]])
    grad_normed1 = sum_over_rows(product_term_back(qkv_gathered, qkv_flat), grid_rows)
    ln1_gain_part = jnp.sum(grad_normed1 * normal1, axis=0)
    ln1_bias_part = jnp.sum(grad_normed1, axis=0)
    input_grad = (
        (grad_hidden + norm_backward(grad_normed1, normal1, inv_std1, ln1_gain))
        .astype(jnp.bfloat16)
        .T
    )
    summed = lax.psum(
        (
            qkv_weight_grad,
            qv_bias_grad,
            out_weight_grad,
            out_bias_grad,
            fc_weight_grad,
            fc_bias_grad,
            proj_weight_grad,
            proj_bias_grad,
        ),
        "dp",
    )
    gain_sums = lax.psum(
        (ln1_gain_part, ln1_bias_part, ln2_gain_part, ln2_bias_part), ("dp", "row")
    )
    return (
        output,
        input_grad,
        gain_sums[0],
        gain_sums[1],
        summed[0],
        summed[1],
        summed[2],
        summed[3],
        gain_sums[2],
        gain_sums[3],
        summed[4],
        summed[5],
        summed[6],
        summed[7],
    )


def solution(mesh):
    return jax.shard_map(
        body,
        mesh=mesh,
        in_specs=(
            P("col", ("dp", "row")),
            P("col"),
            P("col"),
            P("col", None, "row"),
            P(None, "row"),
            P("row", "col"),
            P("col"),
            P("col"),
            P("col"),
            P("col", "row"),
            P("row"),
            P("col", "row"),
            P("col"),
            P(("dp", "col"), None),
            P("col", ("dp", "row")),
        ),
        out_specs=(
            P("col", ("dp", "row")),
            P("col", ("dp", "row")),
            P("col"),
            P("col"),
            P("col", None, "row"),
            P(None, "row"),
            P("row", "col"),
            P("col"),
            P("col"),
            P("col"),
            P("col", "row"),
            P("row"),
            P("col", "row"),
            P("col"),
        ),
        check_vma=False,
    )
```

profile of v0, /device:TPU:0, one launch (start us, length us, event | category | flops | bytes accessed | tf_op | source)
XLA Modules:
  0.0 1619.4 jit_solution(15956005102190218412)
XLA Ops:
  14.6 51.0 %all-gather.10.cloned.1.call-done = bf16[2048,544]{0,1:T(8,128)(2,1)} async-done(((bf16[512,544]{0,1:T(8,128)(2,1)}), bf16[2048,544]{0,1:T(8,128)(2,1)}) %all-gather.10.cloned.1.call-update) | async-done | bytes 2228240 | tf_op jit(solution)/shard_map/all_gather | solution.py:42
  65.5 6.3 fusion.88
  72.6 13.2 reduce-scatter.10.cloned.1.call-done
  92.0 76.8 %all_to_all.60 = bf16[1024,3,272]{2,1,0:T(4,128)(2,1)} all-to-all(bf16[1024,3,272]{2,1,0:T(4,128)(2,1)} %copy.152), channel_id=1, replica_groups=mesh['dp'=4,'row'=4,'col'=2] {'row'}, dimensions={0} | all-to-all | bytes 3342336 | tf_op jit(solution)/shard_map/all_to_all | solution.py:68
  175.9 82.6 %all-gather.12.cloned.1.call-done = bf16[1024,2,17,64]{0,3,2,1:T(8,128)(2,1)} async-done(((bf16[256,2,17,64]{0,3,2,1:T(8,128)(2,1)}), bf16[1024,2,17,64]{0,3,2,1:T(8,128)(2,1)}) %all-gather.12.cloned.1.call-update) | async-done | bytes 4456464 | tf_op jit(solution)/shard_map/all_gather | solution.py:268
  258.5 5.0 copy.198
  263.6 13.0 while.64
  276.7 17.2 %while.65 = (s32[]{:T(128)}, f32[256,17,64]{0,2,1:T(8,128)S(1)}, bf16[2,512,2,17,64]{1,4,3,2,0:T(8,128)(2,1)}, s32[2,512]{1,0:T(2,128)S(1)}, s32[2,512]{1,0:T(2,...) while((s32[]{:T(128)}, f32[256,17,64]{0,2,1:T(8,128)S(1)}, ...), condition=%wide.region_13.14_spmd.clone.clone.clone, body=%wide.region_12.13_spmd.clone.clone.clone.sunk | while | flops 580682752 | bytes 9765531 | solution.py:179
  294.0 6.3 copy.199
  300.8 5.9 reduce.10
  306.9 18.0 %all_to_all.61 = bf16[4,2,34816]{2,1,0:T(2,128)(2,1)S(1)} all-to-all(bf16[4,2,34816]{2,1,0:T(2,128)(2,1)S(1)} %reshape.633), channel_id=1, replica_groups=mesh['dp'=4,'row'=4,'col'=2] {'row'}, dimensions={0} | all-to-all | bytes 1114112 | tf_op jit(solution)/shard_map/all_to_all | solution.py:72
  327.0 8.2 all-gather.14.cloned.1.call-done
  340.5 81.7 %reduce-scatter.12.cloned.1.call-done = f32[512,544]{0,1:T(8,128)} async-done(((f32[2048,544]{0,1:T(8,128)}), f32[512,544]{0,1:T(8,128)}) %reduce-scatter.12.cloned.1.call-update) | async-done | bytes 1114128 | tf_op jit(solution)/shard_map/reduce_scatter | solution.py:50
  427.4 45.1 %all-gather.20.cloned.1.call-done = bf16[2048,544]{0,1:T(8,128)(2,1)} async-done(((bf16[512,544]{0,1:T(8,128)(2,1)}), bf16[2048,544]{0,1:T(8,128)(2,1)}) %all-gather.20.cloned.1.call-update) | async-done | bytes 2228240 | tf_op jit(solution)/shard_map/all_gather | solution.py:42
  472.5 9.1 fusion.83
  481.7 40.3 %all-gather.16.cloned.1.call-done = bf16[2048,544]{0,1:T(8,128)(2,1)} async-done(((bf16[512,544]{0,1:T(8,128)(2,1)}), bf16[2048,544]{0,1:T(8,128)(2,1)}) %all-gather.16.cloned.1.call-update) | async-done | bytes 2228240 | tf_op jit(solution)/shard_map/all_gather | solution.py:42
  521.9 9.2 fusion.82
  531.9 8.6 reduce-scatter.18.cloned.1.call-done
  540.5 21.0 %reduce-scatter.14.cloned.1.call-done = f32[1024,1088]{0,1:T(8,128)} async-done(((f32[2048,1088]{0,1:T(8,128)}), f32[1024,1088]{0,1:T(8,128)}) %reduce-scatter.14.cloned.1.call-update) | async-done | bytes 4456464 | tf_op jit(solution)/shard_map/reduce_scatter | solution.py:59
  561.5 13.7 add_convert_fusion
  575.5 15.3 all-gather.22.cloned.1.call-done
  590.8 6.9 fusion.90
  597.8 82.3 %reduce-scatter.20.cloned.1.call-done = f32[512,544]{0,1:T(8,128)} async-done(((f32[2048,544]{0,1:T(8,128)}), f32[512,544]{0,1:T(8,128)}) %reduce-scatter.20.cloned.1.call-update) | async-done | bytes 1114128 | tf_op jit(solution)/shard_map/reduce_scatter | solution.py:50
  686.3 48.9 %all-gather.24.cloned.1.call-done = bf16[2048,544]{0,1:T(8,128)(2,1)} async-done(((bf16[512,544]{0,1:T(8,128)(2,1)}), bf16[2048,544]{0,1:T(8,128)(2,1)}) %all-gather.24.cloned.1.call-update) | async-done | bytes 2228240 | tf_op jit(solution)/shard_map/all_gather | solution.py:42
  739.4 8.8 reduce-scatter.22.cloned.1.call-done
  753.0 4.8 all-to-all-start.2
  757.9 15.8 all-to-all-done.2
  781.7 14.4 while.66
  796.1 205.7 %while.67 = (s32[]{:T(128)}, f32[256,17,64]{0,2,1:T(8,128)S(1)}, f32[2,512,2,17,64]{1,0,4,3,2:T(2,128)}, bf16[2,512,2,17,64]{1,4,3,2,0:T(8,128)(2,1)}, s32[2,512...) while((s32[]{:T(128)}, f32[256,17,64]{0,2,1:T(8,128)S(1)}, ...), condition=%wide.region_32.33_spmd.clone.clone.clone, body=%wide.region_31.32_spmd.clone.clone.clone.sunk | while | flops 1451361280 | bytes 84034224 | solution.py:224
  810.6 9.2 copy.202
  819.8 79.4 %dynamic_update_slice.10 = f32[2,512,2,17,64]{1,0,4,3,2:T(2,128)} dynamic-update-slice(f32[2,512,2,17,64]{1,0,4,3,2:T(2,128)} %get-tuple-element.1811, f32[1,512,2,17,64]{1,0,4,3,2:T(1,128)} %copy.202, s32[]{:T(128)S(6)} %copy.228, s32[]{:T(128)} %constant.165.clone.1..sunk.3, s32[]{:T(128)} %constant.165.clone.1..sunk.3, s32[]{:T(128)} %constant.165.clone.1..sunk.3, s32[]{:T(128)} %constant.165.clone.1..sunk.3) | dynamic-update-slice | bytes 8912900 | tf_op jit(solution)/shard_map/while/body/jit(dynamic_update_index_in_dim)/dynamic_update_slice | solution.py:224
  913.3 9.2 copy.202
  922.4 79.4 %dynamic_update_slice.10 = f32[2,512,2,17,64]{1,0,4,3,2:T(2,128)} dynamic-update-slice(f32[2,512,2,17,64]{1,0,4,3,2:T(2,128)} %get-tuple-element.1811, f32[1,512,2,17,64]{1,0,4,3,2:T(1,128)} %copy.202, s32[]{:T(128)S(6)} %copy.228, s32[]{:T(128)} %constant.165.clone.1..sunk.3, s32[]{:T(128)} %constant.165.clone.1..sunk.3, s32[]{:T(128)} %constant.165.clone.1..sunk.3, s32[]{:T(128)} %constant.165.clone.1..sunk.3) | dynamic-update-slice | bytes 8912900 | tf_op jit(solution)/shard_map/while/body/jit(dynamic_update_index_in_dim)/dynamic_update_slice | solution.py:224
  1001.9 12.6 reshape.621
  1014.7 151.8 %reduce-scatter.24.cloned.1.call-done = f32[256,2,17,64]{0,3,2,1:T(8,128)} async-done(((f32[1024,2,17,64]{0,3,2,1:T(8,128)}), f32[256,2,17,64]{0,3,2,1:T(8,128)}) %reduce-scatter.24.cloned.1.call-update) | async-done | bytes 2228240 | tf_op jit(solution)/shard_map/reduce_scatter | solution.py:50
  1168.4 8.6 copy.165
  1177.0 55.5 %all_to_all.62 = bf16[256,3,1088]{0,1,2:T(4,128)(2,1)S(1)} all-to-all(bf16[256,3,1088]{0,1,2:T(4,128)(2,1)S(1)} %copy.165), channel_id=1, replica_groups=mesh['dp'=4,'row'=4,'col'=2] {'row'}, dimensions={2} | all-to-all | bytes 3342336 | tf_op jit(solution)/shard_map/all_to_all | solution.py:72
  1235.2 5.6 multiply_convert_fusion
  1240.9 6.1 all-gather.26.cloned.1.call-done
  1246.9 6.5 fusion.84
  1253.5 10.7 all-gather.18.cloned.1.call-done
  1264.2 7.0 fusion.89
  1271.4 8.5 convolution_bitcast_fusion.1
  1279.9 7.0 fusion.87
  1301.1 17.1 %all-reduce.1 = (f32[2,272]{1,0:T(2,128)}, f32[544]{0:T(1024)}, f32[1088]{0:T(1024)}, f32[544]{0:T(1024)}) all-reduce(f32[2,272]{1,0:T(2,128)S(1)} %pad_maximum_fusion.1, f32[544]{0:T(1024)S(1)} %convert_reduce_fusion.3, f32[1088]{0:T(1024)S(1)} %convert_reduce_fusion, ...), channel_id=1, replica_groups=mesh['dp'=4,'row'=4,'col'=2] {'dp'}, use_global_device_ids=true, to_apply=%region_45.46 | all-reduce | flops 2720 | bytes 21760 | tf_op jit(solution)/shard_map/psum | solution.py:331
  1318.2 30.3 %reduce-scatter.26.cloned.1.call-done = f32[512,544]{0,1:T(8,128)} async-done(((f32[2048,544]{0,1:T(8,128)}), f32[512,544]{0,1:T(8,128)}) %reduce-scatter.26.cloned.1.call-update) | async-done | bytes 1114128 | tf_op jit(solution)/shard_map/reduce_scatter | solution.py:50
  1352.8 80.9 %all-reduce = (f32[544]{0:T(1024)}, f32[544]{0:T(1024)}, f32[544]{0:T(1024)}, f32[544]{0:T(1024)}) all-reduce(f32[544]{0:T(1024)S(1)} %get-tuple-element.1254, f32[544]{0:T(1024)S(1)} %get-tuple-element.1259, f32[544]{0:T(1024)S(1)} %copy-done.39, f32[544]{0:T(1024)S(1)} %copy-done.40), channel_id=1, replica_groups=mesh['dp'=4,'row'=4,'col'=2] {'dp','row'}, use_global_device_ids=true, to_apply=%region_40.41 | all-reduce | flops 2176 | bytes 17408 | tf_op jit(solution)/shard_map/psum | solution.py:344
  1438.3 166.2 %all-reduce.9.cloned.1.call-done = (f32[544,3,272]{0,2,1:T(8,128)}, f32[272,544]{1,0:T(8,128)}, f32[544,1088]{1,0:T(8,128)}, f32[544,1088]{1,0:T(8,128)}) async-done(((f32[544,3,272]{0,2,1:T(8,128)}, f32[272,544]{1,0:T(8,128)}, f32[544,1088]{1,0:T(8,128)}, f32[544,1088]{1,0:T(8,128)}), (f32[544,3,272]{0,2,1:T(8,128)}, f32[272,544]{1,0:T(8,128)}, f32[544,1088]{1,0:T(8,128)}, ...) | async-done | bytes 7102480 | tf_op jit(solution)/shard_map/psum | solution.py:331
  (295 shorter events, 167.2 us)
Async XLA Ops:
  7.2 514.8 %copy-start = (bf16[544,1088]{1,0:T(8,128)(2,1)S(1)}, bf16[544,1088]{1,0:T(8,128)(2,1)}, u32[]{:S(2)}) copy-start(bf16[544,1088]{1,0:T(8,128)(2,1)} %param.32) | copy-start | bytes 3551236
  7.2 58.4 %copy-start.50 = (bf16[544,3,272]{0,2,1:T(8,128)(2,1)S(1)}, bf16[544,3,272]{0,2,1:T(8,128)(2,1)}, u32[]{:S(2)}) copy-start(bf16[544,3,272]{0,2,1:T(8,128)(2,1)} %param.26) | copy-start | bytes 2663428
  7.2 58.3 %all-gather.10.cloned.1.call-start = ((), (), s32[]{:S(2)}) async-start(), calls=%async_computation.13 | async-start | bytes 2785280 | tf_op jit(solution)/shard_map/all_gather | solution.py:42
  12.4 59.5 %copy-start.29 = (f32[512]{0:T(512)}, f32[512]{0:T(512)S(1)}, u32[]{:S(2)}) copy-start(f32[512]{0:T(512)S(1)} %get-tuple-element.1389) | copy-start | bytes 6148
  12.4 59.5 %copy-start.31 = (f32[512]{0:T(512)}, f32[512]{0:T(512)S(1)}, u32[]{:S(2)}) copy-start(f32[512]{0:T(512)S(1)} %get-tuple-element.1390) | copy-start | bytes 6148
  14.5 71.3 %reduce-scatter.10.cloned.1.call-start = ((), (), s32[]{:S(2)}) async-start(), calls=%async_computation.14 | async-start | bytes 10027008 | tf_op jit(solution)/shard_map/reduce_scatter | solution.py:59
  71.9 186.6 %all-gather.12.cloned.1.call-start = ((), (), s32[]{:S(2)}) async-start(), calls=%async_computation.15 | async-start | bytes 5570560 | tf_op jit(solution)/shard_map/all_gather | solution.py:268
  174.2 160.9 %all-gather.14.cloned.1.call-start = ((), (), s32[]{:S(2)}) async-start(), calls=%async_computation.16 | async-start | bytes 1671168 | tf_op jit(solution)/shard_map/all_gather | solution.py:46
  326.8 95.4 %reduce-scatter.12.cloned.1.call-start = ((), (), s32[]{:S(2)}) async-start(), calls=%async_computation.17 | async-start | bytes 5570560 | tf_op jit(solution)/shard_map/reduce_scatter | solution.py:50
  339.8 82.4 %copy-start.4 = (bf16[544,512]{1,0:T(8,128)(2,1)S(1)}, bf16[544,512]{1,0:T(8,128)(2,1)}, u32[]{:S(2)}) copy-start(bf16[544,512]{1,0:T(8,128)(2,1)} %param.23) | copy-start | bytes 1671172
  339.9 86.4 %copy-start.22 = (f32[544]{0:T(1024)S(1)}, f32[544]{0:T(1024)}, u32[]{:S(2)}) copy-start(f32[544]{0:T(1024)} %param.30) | copy-start | bytes 6532
  339.9 86.4 %copy-start.42 = (f32[544]{0:T(1024)S(1)}, f32[544]{0:T(1024)}, u32[]{:S(2)}) copy-start(f32[544]{0:T(1024)} %param.31) | copy-start | bytes 6532
  339.9 132.7 %all-gather.20.cloned.1.call-start = ((), (), s32[]{:S(2)}) async-start(), calls=%async_computation.22 | async-start | bytes 2785280 | tf_op jit(solution)/shard_map/all_gather | solution.py:42
  340.5 181.5 %all-gather.16.cloned.1.call-start = ((), (), s32[]{:S(2)}) async-start(), calls=%async_computation.18 | async-start | bytes 2785280 | tf_op jit(solution)/shard_map/all_gather | solution.py:42
  423.8 261.2 %copy-start.2 = (f32[512,544]{0,1:T(8,128)}, f32[512,544]{0,1:T(8,128)S(1)}, u32[]{:S(2)}) copy-start(f32[512,544]{0,1:T(8,128)S(1)} %get-tuple-element.1372) | copy-start | bytes 3342340
  426.3 258.7 %copy-start.24 = (f32[512]{0:T(512)}, f32[512]{0:T(512)S(1)}, u32[]{:S(2)}) copy-start(f32[512]{0:T(512)S(1)} %get-tuple-element.1387) | copy-start | bytes 6148
  426.3 258.8 %copy-start.26 = (f32[512]{0:T(512)}, f32[512]{0:T(512)S(1)}, u32[]{:S(2)}) copy-start(f32[512]{0:T(512)S(1)} %get-tuple-element.1388) | copy-start | bytes 6148
  427.3 113.1 %reduce-scatter.18.cloned.1.call-start = ((), (), s32[]{:S(2)}) async-start(), calls=%async_computation.23 | async-start | bytes 13369344 | tf_op jit(solution)/shard_map/reduce_scatter | solution.py:59
  481.6 79.9 %reduce-scatter.14.cloned.1.call-start = ((), (), s32[]{:S(2)}) async-start(), calls=%async_computation.19 | async-start | bytes 13369344 | tf_op jit(solution)/shard_map/reduce_scatter | solution.py:59
  531.2 59.6 %all-gather.22.cloned.1.call-start = ((), (), s32[]{:S(2)}) async-start(), calls=%async_computation.24 | async-start | bytes 6684672 | tf_op jit(solution)/shard_map/all_gather | solution.py:46
  531.9 43.3 %copy-start.20 = (f32[1088]{0:T(1024)}, f32[1088]{0:T(1024)S(1)}, u32[]{:S(2)}) copy-start(f32[1088]{0:T(1024)S(1)} %convert_element_type.108) | copy-start | bytes 13060
  575.3 104.8 %reduce-scatter.20.cloned.1.call-start = ((), (), s32[]{:S(2)}) async-start(), calls=%async_computation.25 | async-start | bytes 5570560 | tf_op jit(solution)/shard_map/reduce_scatter | solution.py:50
  597.7 87.3 %copy-start.8 = (bf16[544,512]{1,0:T(8,128)(2,1)S(1)}, bf16[544,512]{1,0:T(8,128)(2,1)}, u32[]{:S(2)}) copy-start(bf16[544,512]{1,0:T(8,128)(2,1)} %param.37) | copy-start | bytes 1671172
  597.7 137.5 %all-gather.24.cloned.1.call-start = ((), (), s32[]{:S(2)}) async-start(), calls=%async_computation.26 | async-start | bytes 2785280 | tf_op jit(solution)/shard_map/all_gather | solution.py:42
  685.0 54.4 %copy-start.35 = (f32[512]{0:T(512)}, f32[512]{0:T(512)S(1)}, u32[]{:S(2)}) copy-start(f32[512]{0:T(512)S(1)} %get-tuple-element.1393) | copy-start | bytes 6148
  685.0 54.4 %copy-start.37 = (f32[512]{0:T(512)}, f32[512]{0:T(512)S(1)}, u32[]{:S(2)}) copy-start(f32[512]{0:T(512)S(1)} %get-tuple-element.1394) | copy-start | bytes 6148
  686.3 61.9 %reduce-scatter.22.cloned.1.call-start = ((), (), s32[]{:S(2)}) async-start(), calls=%async_computation.27 | async-start | bytes 3342336 | tf_op jit(solution)/shard_map/reduce_scatter | solution.py:59
  753.0 20.6 %all-to-all-start.2 = ((bf16[4,2,34816]{2,1,0:T(2,128)(2,1)}), bf16[4,2,34816]{2,1,0:T(2,128)(2,1)}, u32[]{:S(2)}, u32[]{:S(2)}) async-start(bf16[4,2,34816]{2,1,0:T(2,128)(2,1)} %reshape.635), calls=%async_computation.9 | async-start | bytes 1114112 | tf_op jit(solution)/shard_map/all_to_all | solution.py:68
  757.9 408.6 %reduce-scatter.24.cloned.1.call-start = ((), (), s32[]{:S(2)}) async-start(), calls=%async_computation.28 | async-start | bytes 11141120 | tf_op jit(solution)/shard_map/reduce_scatter | solution.py:50
  1014.5 232.4 %all-gather.26.cloned.1.call-start = ((), (), s32[]{:S(2)}) async-start(), calls=%async_computation.29 | async-start | bytes 5013504 | tf_op jit(solution)/shard_map/all_gather | solution.py:46
  1235.2 29.0 %all-gather.18.cloned.1.call-start = ((), (), s32[]{:S(2)}) async-start(), calls=%async_computation.20 | async-start | bytes 6684672 | tf_op jit(solution)/shard_map/all_gather | solution.py:46
  1240.8 107.7 %reduce-scatter.26.cloned.1.call-start = ((), (), s32[]{:S(2)}) async-start(), calls=%async_computation.30 | async-start | bytes 5570560 | tf_op jit(solution)/shard_map/reduce_scatter | solution.py:50
  1253.5 181.3 %reduce-scatter.16.cloned.1.call-start = ((), (), s32[]{:S(2)}) async-start(), calls=%async_computation.21 | async-start | bytes 5570560 | tf_op jit(solution)/shard_map/reduce_scatter | solution.py:50
  1271.2 333.3 %all-reduce.9.cloned.1.call-start = ((), (), s32[]{:S(2)}) async-start(), calls=%async_computation.31 | async-start | bytes 15597568 | tf_op jit(solution)/shard_map/psum | solution.py:331
  1300.3 48.2 %copy-start.5 = (bf16[544,512]{1,0:T(8,128)(2,1)S(1)}, bf16[544,512]{1,0:T(8,128)(2,1)}, u32[]{:S(2)}) copy-start(bf16[544,512]{1,0:T(8,128)(2,1)} %param.23) | copy-start | bytes 1671172
  1300.3 48.2 %copy-start.28 = (f32[544]{0:T(1024)S(1)}, f32[544]{0:T(1024)}, u32[]{:S(2)}) copy-start(f32[544]{0:T(1024)} %param.24) | copy-start | bytes 6532
  1300.3 48.2 %copy-start.30 = (f32[512]{0:T(512)S(1)}, f32[512]{0:T(512)}, u32[]{:S(2)}) copy-start(f32[512]{0:T(512)} %copy-done.29) | copy-start | bytes 6148
  1300.3 48.2 %copy-start.32 = (f32[512]{0:T(512)S(1)}, f32[512]{0:T(512)}, u32[]{:S(2)}) copy-start(f32[512]{0:T(512)} %copy-done.31) | copy-start | bytes 6148
  1300.3 52.5 %copy-start.39 = (f32[544]{0:T(1024)S(1)}, f32[544]{0:T(1024)}, u32[]{:S(2)}) copy-start(f32[544]{0:T(1024)} %get-tuple-element.1252) | copy-start | bytes 6532
  1300.3 52.5 %copy-start.40 = (f32[544]{0:T(1024)S(1)}, f32[544]{0:T(1024)}, u32[]{:S(2)}) copy-start(f32[544]{0:T(1024)} %get-tuple-element.1258) | copy-start | bytes 6532
  1300.4 134.4 %copy-start.3 = (f32[512,544]{0,1:T(8,128)S(1)}, f32[512,544]{0,1:T(8,128)}, u32[]{:S(2)}) copy-start(f32[512,544]{0,1:T(8,128)} %copy-done.2) | copy-start | bytes 3342340
  1300.4 134.4 %copy-start.7 = (f32[512,544]{0,1:T(8,128)S(1)}, f32[512,544]{0,1:T(8,128)}, u32[]{:S(2)}) copy-start(f32[512,544]{0,1:T(8,128)} %reduce-scatter.20.cloned.1.call-done) | copy-start | bytes 3342340
  1300.4 134.4 %copy-start.9 = (bf16[544,512]{1,0:T(8,128)(2,1)S(1)}, bf16[544,512]{1,0:T(8,128)(2,1)}, u32[]{:S(2)}) copy-start(bf16[544,512]{1,0:T(8,128)(2,1)} %param.37) | copy-start | bytes 1671172
  1300.4 134.4 %copy-start.23 = (f32[544]{0:T(1024)S(1)}, f32[544]{0:T(1024)}, u32[]{:S(2)}) copy-start(f32[544]{0:T(1024)} %param.30) | copy-start | bytes 6532
  1300.4 134.4 %copy-start.25 = (f32[512]{0:T(512)S(1)}, f32[512]{0:T(512)}, u32[]{:S(2)}) copy-start(f32[512]{0:T(512)} %copy-done.24) | copy-start | bytes 6148
  1300.4 134.4 %copy-start.27 = (f32[512]{0:T(512)S(1)}, f32[512]{0:T(512)}, u32[]{:S(2)}) copy-start(f32[512]{0:T(512)} %copy-done.26) | copy-start | bytes 6148
  1300.4 134.4 %copy-start.36 = (f32[512]{0:T(512)S(1)}, f32[512]{0:T(512)}, u32[]{:S(2)}) copy-start(f32[512]{0:T(512)} %copy-done.35) | copy-start | bytes 6148
  1300.4 134.4 %copy-start.38 = (f32[512]{0:T(512)S(1)}, f32[512]{0:T(512)}, u32[]{:S(2)}) copy-start(f32[512]{0:T(512)} %copy-done.37) | copy-start | bytes 6148
  (24 other events, 112.2 us)
Sparse Core Ops, SparseCore 0:
  14.6 50.8 all-gather.9
  72.0 13.8 reduce-scatter.9
  174.4 84.1 all-gather.11
  326.9 8.2 all-gather.13
  340.0 82.1 reduce-scatter.11
  423.7 48.7 all-gather.19
  474.8 47.1 all-gather.15
  524.3 16.0 reduce-scatter.17
  542.9 18.5 reduce-scatter.13
  575.4 15.3 all-gather.21
  597.8 82.1 reduce-scatter.19
  686.4 48.7 all-gather.23
  739.5 8.6 reduce-scatter.21
  1014.6 151.8 reduce-scatter.23
  1235.3 11.5 all-gather.25
  1248.9 15.2 all-gather.17
  1266.3 82.1 reduce-scatter.25
  1350.7 84.0 reduce-scatter.15
  1439.8 164.6 all-reduce.8
where the time goes:
time: 1640 us; the launch traced here: 1620 us
  waiting for transfers between devices  890 us (54%)
  local copies, waits for them, and re-layouts  264 us (16%)
  blocking collectives  258 us (16%)
  matrix products  113 us (7%)
  other arithmetic  71.5 us (4%)
    reduce_scatter x5, waiting for transfers between devices, sum_over_rows(): lax.psum_scatter(row_term(jnp.int32(0), row_total * lax.axis_size('row'))...  347 us
    all_gather x4, waiting for transfers between devices, gather_rows(): return lax.all_gather(values, 'row', axis=0, tiled=True)  185 us
    dynamic_update_slice x4, local copies, waits for them, and re-layouts, attention_backward(): lax.scan(grad_step, jnp.zeros((query_count, head_count, head_width), jnp....  177 us
    psum x1, waiting for transfers between devices, body(): lax.psum((qkv_weight_grad, qv_bias_grad, out_weight_grad, out_bias_grad,...  166 us
    all_gather x1, waiting for transfers between devices, body(): keyvals = lax.all_gather(local_qkv[:, 1:], 'row', axis=0, tiled=True)  82.6 us
    psum x1, blocking collectives, body(): lax.psum((ln1_gain_part, ln1_bias_part, ln2_gain_part, ln2_bias_part), ('...  80.9 us
    all_to_all x1, blocking collectives, to_heads(): lax.all_to_all(values, 'row', split_axis=0, concat_axis=2, tiled=True)  76.8 us
    all_to_all x2, blocking collectives, to_tokens(): lax.all_to_all(values, 'row', split_axis=2, concat_axis=0, tiled=True)  73.4 us
  transfers between devices with their start and end apart: 20, of which 20 were waited for; matrix products, arithmetic and copies ran while one was open for 5% of the time, Pallas kernels for 0%

commit v1 on v0

--- a/solution.py
+++ b/solution.py
@@ -4,6 +4,8 @@
 import jax
 import jax.numpy as jnp
 from jax import lax
+from jax.experimental import pallas as pl
+from jax.experimental.pallas import tpu as pltpu
 from jax.sharding import PartitionSpec as P
 
 HEAD_DIM = 64
@@ -362,9 +364,967 @@
     )
 
 
+BF = jnp.bfloat16
+F32 = jnp.float32
+MESH = pl.DeviceIdType.MESH
+LANES = 128
+KEY_TILE = 256
+VEC_LN1_GAIN, VEC_LN1_BIAS, VEC_LN2_GAIN, VEC_LN2_BIAS, VEC_OUT_BIAS, VEC_PROJ_BIAS = range(6)
+
+
+def dot_nn(left, right):
+    return lax.dot_general(left, right, (((1,), (0,)), ((), ())), preferred_element_type=F32)
+
+
+def dot_tn(left, right):
+    return lax.dot_general(left, right, (((0,), (0,)), ((), ())), preferred_element_type=F32)
+
+
+def dot_nt(left, right):
+    return lax.dot_general(left, right, (((1,), (1,)), ((), ())), preferred_element_type=F32)
+
+
+VMEM_LIMIT = 66_000_000
+
+
+class Slots:
+    def __init__(self):
+        self.used = 0
+
+    def take(self, count=1):
+        first = self.used
+        self.used += count
+        return first
+
+
+SEND_COUNT, RECV_COUNT, LOCAL_COUNT = 112, 128, 32
+
+
+def layer_kernel(
+    x_in,
+    cot_in,
+    w3_in,
+    ow_in,
+    ff_in,
+    fcb_in,
+    vec_in,
+    doc_in,
+    out_o,
+    ing_o,
+    gf_o,
+    gq_o,
+    vec_o,
+    rf_hbm,
+    rq_hbm,
+    XG,
+    CG,
+    N1,
+    WB,
+    OWB,
+    FB,
+    FCB,
+    FCC,
+    VEC,
+    DOC,
+    MASK,
+    QKV,
+    LSE,
+    ATT,
+    HID,
+    ST1,
+    ST2,
+    N2,
+    ACT,
+    GPRE,
+    PGS,
+    OPS,
+    RCG,
+    RCO,
+    OPO,
+    SZG,
+    RZG,
+    G2,
+    SZO,
+    RZO,
+    RZN,
+    DATT,
+    GQKV,
+    ACCK,
+    ACCV,
+    ZF,
+    DQ,
+    ZQ,
+    ZT,
+    GH,
+    VGC,
+    STX,
+    SPR,
+    SPZ,
+    VOUT,
+    SS,
+    RS,
+    LS,
+    *,
+    doc_count,
+):
+    H, T = x_in.shape
+    R = w3_in.shape[1]
+    HP = w3_in.shape[2]
+    EXT = WB.shape[2]
+    TAIL = EXT - R
+    D = 2 * H
+    S = 2 * T
+    W = KEY_TILE
+    Q = HEAD_DIM
+    FW = ff_in.shape[1]
+    per_tok = T // W
+    n_tiles = S // W
+    inv_d = 1.0 / D
+
+    dp, z, c = lax.axis_index("dp"), lax.axis_index("row"), lax.axis_index("col")
+    oc = 1 - c
+    zz = lax.rem(z, 2)
+    zp = z + 1 - 2 * zz
+    z2 = lax.rem(z + 2, 4)
+    j = lax.rem(z + 2 * c, 4)
+    pair = z // 2
+    core = (dp, z, oc)
+    zdev = (dp, zp, c)
+    xn = dp + 1 - 2 * lax.rem(dp, 2)
+    yn = lax.rem(dp + 2, 4)
+    dg = 3 - dp
+    peers = (dg, xn, yn)
+    first_core, second_core = c == 0, c == 1
+
+    sends, recvs, locs = Slots(), Slots(), Slots()
+    pending = []
+
+    def remote(src, dst, s_idx, r_idx, dev):
+        return pltpu.make_async_remote_copy(
+            src_ref=src,
+            dst_ref=dst,
+            send_sem=SS.at[s_idx],
+            recv_sem=RS.at[r_idx],
+            device_id=dev,
+            device_id_type=MESH,
+        )
+
+    def when(cond, fn):
+        if cond is None:
+            fn()
+        else:
+            pl.when(cond)(fn)
+
+    def push(src, dst, r_idx, dev, cond=None):
+        copy = remote(src, dst, sends.take(), r_idx, dev)
+        when(cond, copy.start)
+        entry = [cond, copy]
+        pending.append(entry)
+        return entry
+
+    def sent(entry):
+        when(entry[0], entry[1].wait_send)
+        pending[:] = [other for other in pending if other is not entry]
+
+    def arrived(dst, r_idx, cond=None):
+        when(cond, remote(dst, dst, 0, r_idx, core).wait_recv)
+
+    def local(src, dst, cond=None):
+        copy = pltpu.make_async_copy(src, dst, LS.at[locs.take()])
+        when(cond, copy.start)
+        return (cond, copy)
+
+    def done(entry):
+        when(entry[0], entry[1].wait)
+
+    barrier = pltpu.get_barrier_semaphore()
+    for step in range(4):
+        for side in range(2):
+            if step == 0 and side == 0:
+                continue
+            target = (dp, lax.rem(z + step, 4), c if side == 0 else oc)
+            pl.semaphore_signal(barrier, inc=1, device_id=target, device_id_type=MESH)
+    for peer in peers:
+        pl.semaphore_signal(barrier, inc=1, device_id=(peer, z, c), device_id_type=MESH)
+    pl.semaphore_wait(barrier, 10)
+
+    r_x_core, r_x_z, r_x_fwd = recvs.take(), recvs.take(), recvs.take()
+    r_w_core, r_w_z, r_w_xy, r_w_tail = recvs.take(), recvs.take(2), recvs.take(4), recvs.take(2)
+    r_vec, r_doc = recvs.take(), recvs.take()
+
+    push(x_in, XG.at[zz, c], r_x_z, zdev)
+    w_row = jnp.minimum(dp, 2)
+    push(w3_in.at[w_row], WB.at[w_row, c, pl.ds(0, R)], r_w_z + c, (dp, z2, 1), dp < 3)
+    has_before = z >= 1
+    push(w3_in.at[:, pl.ds(0, TAIL)], WB.at[:, c, pl.ds(R, TAIL)], r_w_tail + c, (dp, jnp.maximum(z - 1, 0), 0), has_before)
+    push(w3_in.at[:, pl.ds(0, TAIL)], WB.at[:, c, pl.ds(R, TAIL)], r_w_tail + c, (dp, lax.rem(z + 1, 4), 1), has_before)
+    push(x_in, XG.at[zz, c], r_x_core, core)
+    push(w3_in, WB.at[:, 1, pl.ds(0, R)], r_w_core, (dp, z, 0), second_core)
+    push(doc_in, DOC.at[c], r_doc, core)
+    push(vec_in, VEC.at[c], r_vec, core)
+    l_x = local(x_in, XG.at[zz, c])
+    l_w = local(w3_in, WB.at[:, 0, pl.ds(0, R)], first_core)
+    l_doc = local(doc_in, DOC.at[c])
+    l_vec = local(vec_in, VEC.at[c])
+
+    pad_rows = HP - H
+    ones_row = (lax.broadcasted_iota(jnp.int32, (pad_rows, T), 0) == 0).astype(BF)
+    for t in range(2):
+        for h in range(2):
+            N1[t, h, H:, :] = ones_row
+    VGC[...] = jnp.zeros_like(VGC)
+    GQKV[...] = jnp.zeros_like(GQKV)
+
+    def clear_tail():
+        WB[:, :, R:, :] = jnp.zeros((3, 2, TAIL, HP), BF)
+
+    pl.when(j == 3)(clear_tail)
+
+    done(l_doc)
+    arrived(DOC.at[oc], r_doc)
+    lengths = DOC[pair][0:1, :]
+    place_c = lax.broadcasted_iota(jnp.int32, (S, LANES), 0).astype(F32)
+    place_r = lax.broadcasted_iota(jnp.int32, (8, S), 1).astype(F32)
+    end = jnp.zeros((1, 1), F32)
+    seg_c, seg_r = jnp.zeros_like(place_c), jnp.zeros_like(place_r)
+    for number in range(doc_count):
+        end = end + lengths[:, number : number + 1]
+        seg_c = seg_c + jnp.where(end <= place_c, 1.0, 0.0)
+        seg_r = seg_r + jnp.where(end <= place_r, 1.0, 0.0)
+    seg_c = jnp.where(end <= place_c, place_c + 2.0 * S, seg_c)
+    seg_r = jnp.where(end <= place_r, place_r + 2.0 * S, seg_r)
+    for tile in range(n_tiles):
+        rows = W * (tile + 1)
+        first = W * tile * (tile + 1) // 2
+        cols = slice(tile * W, (tile + 1) * W)
+        key_seg = jnp.concatenate([seg_c[:rows]] * (W // LANES), axis=1)
+        key_place = jnp.concatenate([place_c[:rows]] * (W // LANES), axis=1)
+        ok = (key_seg == seg_r[0:1, cols]) & (key_place <= place_r[0:1, cols])
+        MASK[first : first + rows, :] = jnp.where(ok, 0.0, masked_fill)
+
+    done(l_vec)
+    arrived(VEC.at[oc], r_vec)
+
+    def column(h, which):
+        return VEC[h, :, which : which + 1]
+
+    def stats_of(first_half, second_half):
+        center = (
+            jnp.sum(first_half, axis=0, keepdims=True) + jnp.sum(second_half, axis=0, keepdims=True)
+        ) * inv_d
+        square = (
+            jnp.sum(first_half * first_half, axis=0, keepdims=True)
+            + jnp.sum(second_half * second_half, axis=0, keepdims=True)
+        ) * inv_d
+        return center, lax.rsqrt(square - center * center + epsilon)
+
+    def first_norm(t):
+        halves = [XG[t, h].astype(F32) for h in range(2)]
+        center, inv_std = stats_of(*halves)
+        ST1[t, 0:1, :] = center
+        ST1[t, 1:2, :] = inv_std
+        for h in range(2):
+            shaped = (halves[h] - center) * inv_std * column(h, VEC_LN1_GAIN) + column(
+                h, VEC_LN1_BIAS
+            )
+            N1[t, h, 0:H, :] = shaped.astype(BF)
+
+    done(l_x)
+    arrived(XG.at[zz, oc], r_x_core)
+    first_norm(zz)
+
+    w_from_z = second_core & (dp < 3)
+    for h in range(2):
+        arrived(WB.at[w_row, h, pl.ds(0, R)], r_w_z + h, w_from_z)
+    for peer in peers:
+        push(
+            WB.at[w_row, :, pl.ds(0, R)],
+            WB.at[w_row, :, pl.ds(0, R)],
+            r_w_xy + w_row,
+            (peer, z, 1),
+            w_from_z,
+        )
+    arrived(XG.at[1 - zz, c], r_x_z)
+    e_xf = push(XG.at[1 - zz, c], XG.at[1 - zz, c], r_x_fwd, core)
+
+    quarter = ff_in.shape[0] // 4
+    my_quarter = pl.ds(pl.multiple_of(dp * quarter, 16), quarter)
+    r_f_core, r_f_z, r_f_xy, r_fcb = recvs.take(), recvs.take(2), recvs.take(4), recvs.take()
+    push(ff_in.at[my_quarter], FB.at[c, my_quarter], r_f_z + c, (dp, z2, 1))
+    push(ff_in, FB.at[1], r_f_core, (dp, z, 0), second_core)
+    push(fcb_in, FCB, r_fcb, (dp, z2, 1), first_core)
+    l_f = local(ff_in, FB.at[0], first_core)
+    l_fcb = local(fcb_in, FCB, first_core)
+
+    arrived(XG.at[1 - zz, oc], r_x_fwd)
+    first_norm(1 - zz)
+
+    done(l_w)
+    arrived(WB.at[:, 1, pl.ds(0, R)], r_w_core, first_core)
+    for m in range(3):
+        arrived(WB.at[m, :, pl.ds(0, R)], r_w_xy + m, second_core & (dp != m))
+    for h in range(2):
+        arrived(WB.at[:, h, pl.ds(R, TAIL)], r_w_tail + h, j < 3)
+
+    for t in range(2):
+        for m in range(3):
+            mixed = dot_nn(WB[m, 0], N1[t, 0]) + dot_nn(WB[m, 1], N1[t, 1])
+            low = mixed.astype(BF)
+            if m == 0:
+                low = low * jnp.asarray(score_scale, BF)
+            QKV[m, :, t * T : (t + 1) * T] = low
+
+    r_o_core, r_o_z, r_o_fwd = recvs.take(), recvs.take(4), recvs.take(4)
+    r_c_core, r_c_z, r_c_fwd = recvs.take(), recvs.take(), recvs.take()
+
+    def block(number):
+        return pl.ds(pl.multiple_of(number * R, 16), R)
+
+    for step in (1, 3, 2):
+        push(ow_in, OWB.at[c, block(z)], r_o_z + z, (dp, lax.rem(z + step, 4), c))
+    push(cot_in, CG.at[zz, c], r_c_z, zdev)
+    push(ow_in, OWB.at[c, block(z)], r_o_core, core)
+    push(cot_in, CG.at[zz, c], r_c_core, core)
+    l_o = local(ow_in, OWB.at[c, block(z)])
+    l_c = local(cot_in, CG.at[zz, c])
+
+    r_a_z, r_a_core, r_a_fwd = recvs.take(5), recvs.take(5), recvs.take(5)
+    s_a_z, s_a_core, s_a_fwd = sends.take(5), sends.take(5), sends.take(5)
+    first_slot = jnp.where(j == 0, 0, 1)
+
+    def head_rows(owner, slot):
+        return pl.ds(pl.multiple_of(owner * (4 * Q) + slot * Q, Q), Q)
+
+    def slot_rows(slot):
+        return pl.ds(pl.multiple_of(slot * Q - 16 * j, 16), Q)
+
+    def att_copy(owner, slot, s_base, r_base, dev):
+        rows = head_rows(owner, slot)
+        return remote(ATT.at[rows], ATT.at[rows], s_base + slot, r_base + slot, dev)
+
+    forward_slot = 3
+    s_f_xy = sends.take(3)
+
+    def ff_copy(number):
+        part = FB.at[:, my_quarter]
+        return remote(part, part, s_f_xy + number, r_f_xy + dp, (peers[number], z, 1))
+
+    def forward_ff():
+        for h in range(2):
+            arrived(FB.at[h, my_quarter], r_f_z + h, second_core)
+        for number in range(3):
+            when(second_core, ff_copy(number).start)
+
+    def attend(slot, carry):
+        rows = slot_rows(slot)
+        out_rows = head_rows(j, slot)
+        queries = QKV[0, rows, :]
+        keys = QKV[1, rows, :].T
+        values = QKV[2, rows, :]
+        for tile in range(n_tiles):
+            count = W * (tile + 1)
+            first = W * tile * (tile + 1) // 2
+            cols = slice(tile * W, (tile + 1) * W)
+            scores = dot_nn(keys[:count], queries[:, cols]) + MASK[first : first + count, :]
+            best = jnp.max(scores, axis=0, keepdims=True)
+            weights = jnp.exp(scores - best)
+            mass = jnp.sum(weights, axis=0, keepdims=True)
+            probs_low = (weights * (1.0 / mass)).astype(BF)
+            ATT[out_rows, cols] = dot_nn(values[:, :count], probs_low).astype(BF)
+            LSE[slot, 0:1, cols] = best + jnp.log(mass)
+        att_copy(j, slot, s_a_z, r_a_z, zdev).start()
+        att_copy(j, slot, s_a_core, r_a_core, core).start()
+
+        @pl.when(slot == forward_slot)
+        def _():
+            forward_ff()
+
+        return carry
+
+    lax.fori_loop(first_slot, 5, attend, 0)
+
+    arrived(CG.at[1 - zz, c], r_c_z)
+    push(CG.at[1 - zz, c], CG.at[1 - zz, c], r_c_fwd, core)
+    for step in (1, 3, 2):
+        there = lax.rem(z + step, 4)
+        arrived(OWB.at[c, block(there)], r_o_z + there)
+        push(OWB.at[c, block(there)], OWB.at[c, block(there)], r_o_fwd + there, core)
+
+    def owner_of(zv, cv):
+        return lax.rem(zv + 2 * cv, 4)
+
+    def slots_of(owner, body):
+        lax.fori_loop(jnp.where(owner == 0, 0, 1), 5, lambda slot, carry: (body(slot), carry)[1], 0)
+
+    def pass_on(slot):
+        att_copy(owner_of(zp, c), slot, s_a_fwd, r_a_z, core).wait_recv()
+        att_copy(owner_of(zp, c), slot, s_a_fwd, r_a_fwd, core).start()
+
+    slots_of(owner_of(zp, c), pass_on)
+    slots_of(owner_of(z, oc), lambda slot: att_copy(owner_of(z, oc), slot, s_a_core, r_a_core, core).wait_recv())
+    slots_of(owner_of(zp, oc), lambda slot: att_copy(owner_of(zp, oc), slot, s_a_fwd, r_a_fwd, core).wait_recv())
+    done(l_o)
+    arrived(OWB.at[oc, block(z)], r_o_core)
+    for step in range(1, 4):
+        there = lax.rem(z + step, 4)
+        arrived(OWB.at[oc, block(there)], r_o_fwd + there)
+
+    def project(tile, carry):
+        t = tile // per_tok
+        cols = pl.ds(pl.multiple_of(lax.rem(tile, per_tok) * W, W), W)
+        all_cols = pl.ds(pl.multiple_of(tile * W, W), W)
+        att = ATT[:, all_cols]
+        halves = []
+        for h in range(2):
+            branch = dot_tn(OWB[h], att)
+            halves.append(XG[t, h, :, cols].astype(F32) + (branch + column(h, VEC_OUT_BIAS)))
+            HID[t, h, :, cols] = halves[h]
+        center, inv_std = stats_of(*halves)
+        ST2[t, 0:1, cols] = center
+        ST2[t, 1:2, cols] = inv_std
+        for h in range(2):
+            shaped = (halves[h] - center) * inv_std * column(h, VEC_LN2_GAIN) + column(
+                h, VEC_LN2_BIAS
+            )
+            N2[t, h, :, cols] = shaped.astype(BF)
+        return carry
+
+    lax.fori_loop(0, n_tiles, project, 0)
+
+    done(l_f)
+    done(l_fcb)
+    arrived(FB.at[1], r_f_core, first_core)
+    arrived(FCB, r_fcb, second_core)
+    for number in range(4):
+        rows = pl.ds(number * quarter, quarter)
+        arrived(FB.at[:, rows], r_f_xy + number, second_core & (dp != number))
+    done(l_c)
+    arrived(CG.at[zz, oc], r_c_core)
+    arrived(CG.at[1 - zz, oc], r_c_fwd)
+
+    one_row = (lax.broadcasted_iota(jnp.int32, (16, LANES), 0) == 0).astype(BF)
+    FCC[...] = dot_tn(FCB[...], one_row)
+
+    r_g_core, r_p_core, r_g_z = recvs.take(n_tiles), recvs.take(n_tiles), recvs.take(n_tiles)
+    s_g_core, s_p_core, s_g_z = sends.take(n_tiles), sends.take(n_tiles), sends.take(n_tiles)
+
+    def tile_at(tile):
+        t = tile // per_tok
+        return t, pl.ds(pl.multiple_of(lax.rem(tile, per_tok) * W, W), W)
+
+    def part_copy(buf, dst, tile, s_base, r_base, dev):
+        t, cols = tile_at(tile)
+        return remote(buf.at[t, :, cols], dst.at[t, :, cols], s_base + tile, r_base + tile, dev)
+
+    def feed(tile, carry):
+        t, cols = tile_at(tile)
+        all_cols = pl.ds(pl.multiple_of(tile * W, W), W)
+        pre = (
+            dot_tn(FB[0, 0:H], N2[t, 0, :, cols])
+            + dot_tn(FB[1, 0:H], N2[t, 1, :, cols])
+            + FCC[:, 0:1]
+        )
+        phi = 0.5 * (1.0 + lax.erf(pre * (2.0**-0.5)))
+        ACT[:, all_cols] = (pre * phi).astype(BF)
+        slope = phi + pre * jnp.exp(pre * pre * -0.5) * ((2.0 * math.pi) ** -0.5)
+        grad_act = dot_tn(FB[0, H:D], CG[t, 0, :, cols]) + dot_tn(FB[1, H:D], CG[t, 1, :, cols])
+        GPRE[:, all_cols] = (grad_act * slope).astype(BF)
+        PGS[t, :, cols] = dot_nn(FB[oc, 0:H], GPRE[:, all_cols]).astype(BF)
+        part_copy(PGS, RCG, tile, s_g_core, r_g_core, core).start()
+        own = dot_nn(FB[c, 0:H], GPRE[:, all_cols])
+        OPS[t, :, cols] = dot_nn(FB[oc, H:D], ACT[:, all_cols]).astype(BF)
+        part_copy(OPS, RCO, tile, s_p_core, r_p_core, core).start()
+        part_copy(PGS, RCG, tile, s_g_core, r_g_core, core).wait_recv()
+        SZG[t, :, cols] = (own + RCG[t, :, cols].astype(F32)).astype(BF)
+        part_copy(SZG, RZG, tile, s_g_z, r_g_z, zdev).start()
+        OPO[t, :, cols] = dot_nn(FB[c, H:D], ACT[:, all_cols]).astype(BF)
+        return carry
+
+    lax.fori_loop(0, n_tiles, feed, 0)
+
+    def wait_sends(tile, carry):
+        part_copy(PGS, RCG, tile, s_g_core, r_g_core, core).wait_send()
+        part_copy(OPS, RCO, tile, s_p_core, r_p_core, core).wait_send()
+        return carry
+
+    r_out_z = recvs.take()
+
+    def wait_out(tile, carry):
+        part_copy(OPS, RCO, tile, s_p_core, r_p_core, core).wait_recv()
+        return carry
+
+    lax.fori_loop(0, n_tiles, wait_out, 0)
+    SZO[...] = (OPO[1 - zz].astype(F32) + RCO[1 - zz].astype(F32)).astype(BF)
+    push(SZO, RZO, r_out_z, zdev)
+
+    for number in range(3):
+        when(second_core, ff_copy(number).wait_send)
+    r_rf = recvs.take(4)
+    rf_entries = []
+    for number in range(4):
+        rows = slice(number * quarter, (number + 1) * quarter)
+        for h in range(2):
+            if number < 2:
+                left, right, low = N2, GPRE, number * quarter
+            else:
+                left, right, low = CG, ACT, (number - 2) * quarter
+            total = dot_nt(left[0, h, low : low + quarter, :], right[:, 0:T]) + dot_nt(
+                left[1, h, low : low + quarter, :], right[:, T:S]
+            )
+            FB[h, rows, :] = total.astype(BF)
+        rf_entries.append(
+            push(
+                FB.at[:, pl.ds(number * quarter, quarter)],
+                rf_hbm.at[dp],
+                r_rf + dp,
+                (number, z, c),
+                dp != number,
+            )
+        )
+    SPR[dp] = jnp.zeros(SPR.shape[1:], F32)
+    SPR[dp, 6:7, :] = dot_nt(jnp.ones((16, S), BF), GPRE[...])[0:1, :]
+
+    r_g_all = recvs.take(n_tiles)
+    s_g_all = sends.take(n_tiles)
+
+    def g2_copy(tile):
+        t, cols = tile_at(tile)
+        return remote(G2.at[t, c, :, cols], G2.at[t, c, :, cols], s_g_all + tile, r_g_all + tile, core)
+
+    def g2_other(tile):
+        t, cols = tile_at(tile)
+        return remote(G2.at[t, oc, :, cols], G2.at[t, oc, :, cols], s_g_all + tile, r_g_all + tile, core)
+
+    def join(tile, carry):
+        t, cols = tile_at(tile)
+        part_copy(SZG, RZG, tile, s_g_z, r_g_z, zdev).wait_recv()
+        G2[t, c, :, cols] = (SZG[t, :, cols].astype(F32) + RZG[t, :, cols].astype(F32)).astype(BF)
+        g2_copy(tile).start()
+        return carry
+
+    lax.fori_loop(0, n_tiles, join, 0)
+
+    def norm_back(grads, normals, inv_std, gain_index):
+        scaled = [grads[h] * column(h, gain_index) for h in range(2)]
+        plain = sum(jnp.sum(scaled[h], axis=0, keepdims=True) for h in range(2)) * inv_d
+        cross = sum(jnp.sum(scaled[h] * normals[h], axis=0, keepdims=True) for h in range(2)) * inv_d
+        return [inv_std * (scaled[h] - plain - normals[h] * cross) for h in range(2)]
+
+    def second_back(tile, carry):
+        t, cols = tile_at(tile)
+        g2_other(tile).wait_recv()
+        center, inv_std = ST2[t, 0:1, cols], ST2[t, 1:2, cols]
+        grads = [G2[t, h, :, cols].astype(F32) for h in range(2)]
+        normals = [(HID[t, h, :, cols] - center) * inv_std for h in range(2)]
+        back = norm_back(grads, normals, inv_std, VEC_LN2_GAIN)
+        for h in range(2):
+            grad_hidden = CG[t, h, :, cols].astype(F32) + back[h]
+            XG[t, h, :, cols] = grad_hidden.astype(BF)
+
+            @pl.when((t == zz) & (c == h))
+            def _():
+                GH[:, cols] = grad_hidden
+                VGC[:, 2:3] = VGC[:, 2:3] + jnp.sum(grads[h] * normals[h], axis=1, keepdims=True)
+                VGC[:, 3:4] = VGC[:, 3:4] + jnp.sum(grads[h], axis=1, keepdims=True)
+
+        return carry
+
+    sent(e_xf)
+    lax.fori_loop(0, n_tiles, second_back, 0)
+    GB = XG
+    VGC[:, 4:5] = jnp.sum(GB[zz, c].astype(F32), axis=1, keepdims=True)
+    VGC[:, 5:6] = jnp.sum(CG[zz, c].astype(F32), axis=1, keepdims=True)
+
+    window = pl.ds(pl.multiple_of(j * (4 * Q), Q), 5 * Q)
+    for t in range(2):
+        DATT[:, t * T : (t + 1) * T] = (
+            dot_nn(OWB[0, window, :], GB[t, 0]) + dot_nn(OWB[1, window, :], GB[t, 1])
+        ).astype(BF)
+    r_rq = recvs.take(4)
+    rq_entries = []
+    for h in range(2):
+        total = dot_nt(ATT[block(j), 0:T], GB[0, h]) + dot_nt(ATT[block(j), T:S], GB[1, h])
+        DQ[3, h, 0:R, 0:H] = total.astype(BF)
+    rq_entries.append(push(DQ.at[3], rq_hbm.at[dp], r_rq + dp, (3, z, c), dp != 3))
+    l_x2 = local(x_in, XG.at[zz, c])
+
+    def attend_back(slot, carry):
+        rows = slot_rows(slot)
+        here = pl.ds(pl.multiple_of(slot * Q, Q), Q)
+        queries = QKV[0, rows, :]
+        keys_t = QKV[1, rows, :]
+        keys = keys_t.T
+        values = QKV[2, rows, :].T
+        grads_out = DATT[here, :]
+        for tile in reversed(range(n_tiles)):
+            count = W * (tile + 1)
+            first = W * tile * (tile + 1) // 2
+            cols = slice(tile * W, (tile + 1) * W)
+            scores = dot_nn(keys[:count], queries[:, cols]) + MASK[first : first + count, :]
+            probs = jnp.exp(scores - LSE[slot, 0:1, cols])
+            grad_probs = dot_nn(values[:count], grads_out[:, cols])
+            delta = jnp.sum(probs * grad_probs, axis=0, keepdims=True)
+            grad_scores = (probs * (grad_probs - delta)).astype(BF)
+            probs_low = probs.astype(BF)
+            part_v = dot_nt(grads_out[:, cols], probs_low)
+            part_k = dot_nt(queries[:, cols], grad_scores)
+            if tile == n_tiles - 1:
+                ACCV[...] = part_v
+                ACCK[...] = part_k
+            else:
+                ACCV[:, 0:count] = ACCV[:, 0:count] + part_v
+                ACCK[:, 0:count] = ACCK[:, 0:count] + part_k
+            GQKV[0, rows, cols] = (dot_nn(keys_t[:, :count], grad_scores) * score_scale).astype(BF)
+        GQKV[1, rows, :] = ACCK[...].astype(BF)
+        GQKV[2, rows, :] = ACCV[...].astype(BF)
+        return carry
+
+    lax.fori_loop(first_slot, 5, attend_back, 0)
+
+    for m in range(3):
+        for h in range(2):
+            total = dot_nt(GQKV[m, :, 0:T], N1[0, h]) + dot_nt(GQKV[m, :, T:S], N1[1, h])
+            DQ[m, h] = total.astype(BF)
+        rq_entries.append(push(DQ.at[m], rq_hbm.at[dp], r_rq + dp, (m, z, c), dp != m))
+
+    def wait_sends(tile, carry):
+        part_copy(PGS, RCG, tile, s_g_core, r_g_core, core).wait_send()
+        part_copy(OPS, RCO, tile, s_p_core, r_p_core, core).wait_send()
+        part_copy(SZG, RZG, tile, s_g_z, r_g_z, zdev).wait_send()
+        g2_copy(tile).wait_send()
+        return carry
+
+    lax.fori_loop(0, n_tiles, wait_sends, 0)
+    r_n_core, r_n_z = recvs.take(n_tiles), recvs.take()
+    s_n_core = sends.take(n_tiles)
+
+    def back_rows(half, tile):
+        all_cols = pl.ds(pl.multiple_of(tile * W, W), W)
+        total = dot_tn(WB[0, half, :, 0:H], GQKV[0, :, all_cols])
+        for m in range(1, 3):
+            total = total + dot_tn(WB[m, half, :, 0:H], GQKV[m, :, all_cols])
+        return total
+
+    def first_part(tile, carry):
+        t, cols = tile_at(tile)
+        PGS[t, :, cols] = back_rows(oc, tile).astype(BF)
+        part_copy(PGS, RCG, tile, s_n_core, r_n_core, core).start()
+        OPS[t, :, cols] = back_rows(c, tile).astype(BF)
+        return carry
+
+    lax.fori_loop(0, n_tiles, first_part, 0)
+
+    def wait_first(tile, carry):
+        part_copy(PGS, RCG, tile, s_n_core, r_n_core, core).wait_recv()
+        return carry
+
+    lax.fori_loop(0, n_tiles, wait_first, 0)
+    SZG[0] = (OPS[1 - zz].astype(F32) + RCG[1 - zz].astype(F32)).astype(BF)
+    push(SZG.at[0], RZN, r_n_z, zdev)
+
+    for entry in rf_entries:
+        sent(entry)
+    loads = []
+    for number in range(4):
+        other = dp != number
+        arrived(rf_hbm.at[number], r_rf + number, other)
+        loads.append(
+            local(rf_hbm.at[number], FB.at[:, pl.ds(number * quarter, quarter)], other)
+        )
+    for entry in loads:
+        done(entry)
+    r_zf = recvs.take(2)
+    first_rows = slice(0, quarter)
+    for h in range(2):
+        total = FB[h, 0:quarter, :].astype(F32)
+        for number in range(1, 4):
+            total = total + FB[h, number * quarter : (number + 1) * quarter, :].astype(F32)
+        low = total.astype(BF)
+        FB[h, 0:quarter, :] = low
+        if h == 0:
+
+            @pl.when(first_core)
+            def _():
+                ZF[0] = low
+
+        push(FB.at[h, pl.ds(0, quarter)], ZF.at[1], r_zf + 1, (dp, z2, h), second_core)
+        if h == 1:
+            push(FB.at[h, pl.ds(0, quarter)], ZF.at[0], r_zf, (dp, z, 1), first_core)
+
+    arrived(RZO, r_out_z)
+    branch_out = OPO[zz].astype(F32) + RCO[zz].astype(F32) + RZO[...].astype(F32)
+    OPO[0] = (HID[zz, c] + branch_out + VEC[c, :, VEC_PROJ_BIAS : VEC_PROJ_BIAS + 1]).astype(BF)
+    l_out = local(OPO.at[0], out_o)
+
+    done(l_x2)
+    arrived(RZN, r_n_z)
+    r_stat = recvs.take()
+    grads = OPS[zz].astype(F32) + RCG[zz].astype(F32) + RZN[...].astype(F32)
+    center, inv_std = ST1[zz, 0:1, :], ST1[zz, 1:2, :]
+    normals = (XG[zz, c].astype(F32) - center) * inv_std
+    scaled = grads * VEC[c, :, VEC_LN1_GAIN : VEC_LN1_GAIN + 1]
+    STX[c, 0:1, :] = jnp.sum(scaled, axis=0, keepdims=True)
+    STX[c, 1:2, :] = jnp.sum(scaled * normals, axis=0, keepdims=True)
+    push(STX.at[c], STX.at[c], r_stat, core)
+    VGC[:, 0:1] = jnp.sum(grads * normals, axis=1, keepdims=True)
+    VGC[:, 1:2] = jnp.sum(grads, axis=1, keepdims=True)
+    arrived(STX.at[oc], r_stat)
+    sums = (STX[0] + STX[1]) * inv_d
+    OPO[1] = (GH[...] + inv_std * (scaled - sums[0:1] - normals * sums[1:2])).astype(BF)
+    l_ing = local(OPO.at[1], ing_o)
+
+    r_sp, r_spz = recvs.take(4), recvs.take(8)
+    turned = VGC[...].T
+    SPR[dp, 0:6, 0:H] = turned[0:6, :]
+    for peer in peers:
+        push(SPR.at[dp], SPR.at[dp], r_sp + dp, (peer, z, c))
+
+    for entry in rq_entries:
+        sent(entry)
+    loads = []
+    for number in range(4):
+        other = dp != number
+        arrived(rq_hbm.at[number], r_rq + number, other)
+        loads.append(local(rq_hbm.at[number], DQ.at[number], other))
+    for entry in loads:
+        done(entry)
+    r_zq, r_zt = recvs.take(2), recvs.take(2)
+    with_tail = (j < 3) & (dp < 3)
+    next_block = jnp.minimum(j + 1, 3)
+    for h in range(2):
+        total = DQ[0, h].astype(F32)
+        for number in range(1, 4):
+            total = total + DQ[number, h].astype(F32)
+        low = total.astype(BF)
+        DQ[0, h] = low
+        if h == 0:
+
+            @pl.when(first_core)
+            def _():
+                ZQ[0] = low[0:R]
+
+        push(DQ.at[0, h, pl.ds(0, R)], ZQ.at[1], r_zq + 1, (dp, z2, h), second_core)
+        if h == 1:
+            push(DQ.at[0, h, pl.ds(0, R)], ZQ.at[0], r_zq, (dp, z, 1), first_core)
+        push(DQ.at[0, h, pl.ds(R, TAIL)], ZT.at[c], r_zt + c, (dp, next_block, h), with_tail)
+
+    r_gf, r_gq = recvs.take(4), recvs.take(4)
+    arrived(ZF.at[0], r_zf, second_core)
+    arrived(ZF.at[1], r_zf + 1)
+    ZF[0] = (ZF[0].astype(F32) + ZF[1].astype(F32)).astype(BF)
+    l_gf = local(ZF.at[0], gf_o.at[my_quarter])
+    for peer in peers:
+        push(ZF.at[0], gf_o.at[my_quarter], r_gf + dp, (peer, z, c))
+
+    for number in range(4):
+        arrived(SPR.at[number], r_sp + number, dp != number)
+    SPZ[z, c] = SPR[0] + SPR[1] + SPR[2] + SPR[3]
+    for step in range(4):
+        for side in range(2):
+            if step == 0 and side == 0:
+                continue
+            target = (dp, lax.rem(z + step, 4), c if side == 0 else oc)
+            push(SPZ.at[z, c], SPZ.at[z, c], r_spz + (2 * z + c), target)
+
+    arrived(ZQ.at[0], r_zq, second_core)
+    arrived(ZQ.at[1], r_zq + 1)
+    gets_tail = (z >= 1) & (dp < 3)
+    for side in range(2):
+        arrived(ZT.at[side], r_zt + side, gets_tail)
+    total = ZQ[0].astype(F32) + ZQ[1].astype(F32)
+    ZQ[0] = total.astype(BF)
+
+    @pl.when(gets_tail)
+    def _():
+        ZQ[0, 0:TAIL] = (total[0:TAIL] + ZT[0].astype(F32) + ZT[1].astype(F32)).astype(BF)
+
+    l_gq = local(ZQ.at[0], gq_o.at[dp])
+    for peer in peers:
+        push(ZQ.at[0], gq_o.at[dp], r_gq + dp, (peer, z, c))
+
+    for step in range(4):
+        for side in range(2):
+            if step == 0 and side == 0:
+                continue
+            zv, cv = lax.rem(z + step, 4), c if side == 0 else oc
+            arrived(SPZ.at[zv, cv], r_spz + (2 * zv + cv))
+    vectors = SPZ[0, c] + SPZ[1, c] + SPZ[2, c] + SPZ[3, c]
+    VOUT[...] = vectors
+    VOUT[6:7, :] = SPZ[z, 0, 6:7, :] + SPZ[z2, 1, 6:7, :]
+    l_vec_o = local(VOUT, vec_o)
+
+    for number in range(4):
+        arrived(gf_o.at[pl.ds(number * quarter, quarter)], r_gf + number, dp != number)
+        arrived(gq_o.at[number], r_gq + number, dp != number)
+    for entry in (l_out, l_ing, l_gf, l_gq, l_vec_o):
+        done(entry)
+
+    def own_sends(slot):
+        att_copy(j, slot, s_a_z, r_a_z, zdev).wait_send()
+        att_copy(j, slot, s_a_core, r_a_core, core).wait_send()
+
+    slots_of(j, own_sends)
+    slots_of(
+        owner_of(zp, c),
+        lambda slot: att_copy(owner_of(zp, c), slot, s_a_fwd, r_a_fwd, core).wait_send(),
+    )
+
+    def last_sends(tile, carry):
+        part_copy(PGS, RCG, tile, s_n_core, r_n_core, core).wait_send()
+        return carry
+
+    lax.fori_loop(0, n_tiles, last_sends, 0)
+    for entry in list(pending):
+        sent(entry)
+    assert sends.used <= SEND_COUNT and recvs.used <= RECV_COUNT and locs.used <= LOCAL_COUNT
+
+
+def fast_body(
+    tokens,
+    ln1_gain,
+    ln1_bias,
+    qkv_weight,
+    qv_bias,
+    out_weight,
+    out_bias,
+    ln2_gain,
+    ln2_bias,
+    fc_weight,
+    fc_bias,
+    proj_weight,
+    proj_bias,
+    doc_lengths,
+    cotangent,
+):
+    H, T = tokens.shape
+    R = out_weight.shape[0]
+    FW = fc_weight.shape[1]
+    D, S = 2 * H, 2 * T
+    HP = (H // LANES + 1) * LANES
+    EXT = 5 * HEAD_DIM
+    NT = S // KEY_TILE
+    doc_count = doc_lengths.shape[1]
+    first_core = lax.axis_index("col") == 0
+    low_bias = jnp.where(first_core, qv_bias, jnp.zeros_like(qv_bias))
+    bias_three = jnp.stack([low_bias[0], jnp.zeros_like(low_bias[0]), low_bias[1]])
+    w3 = jnp.concatenate(
+        [
+            jnp.transpose(qkv_weight, (1, 2, 0)),
+            bias_three[:, :, None],
+            jnp.zeros((3, R, HP - H - 1), BF),
+        ],
+        axis=2,
+    )
+    ff = jnp.concatenate([fc_weight, proj_weight], axis=0)
+    fcb = jnp.pad(fc_bias[None], ((0, 15), (0, 0)))
+    vec = jnp.stack(
+        [ln1_gain, ln1_bias, ln2_gain, ln2_bias, out_bias.astype(F32), proj_bias.astype(F32)], axis=1
+    )
+    vec = jnp.pad(vec, ((0, 0), (0, LANES - 6)))
+    doc = jnp.pad(doc_lengths.astype(F32), ((0, 7), (0, LANES - doc_count)))
+    shape = jax.ShapeDtypeStruct
+    anywhere = pl.BlockSpec(memory_space=pl.ANY)
+    outs = [
+        shape((H, T), BF),
+        shape((H, T), BF),
+        shape((2 * H, FW), BF),
+        shape((4, R, HP), BF),
+        shape((8, FW), F32),
+        shape((4, 2, 2 * H // 4, FW), BF),
+        shape((4, 2, EXT, HP), BF),
+    ]
+    vmem = pltpu.VMEM
+    mask_rows = KEY_TILE * NT * (NT + 1) // 2
+    scratch = [
+        vmem((2, 2, H, T), BF),
+        vmem((2, 2, H, T), BF),
+        vmem((2, 2, HP, T), BF),
+        vmem((3, 2, EXT, HP), BF),
+        vmem((2, D, H), BF),
+        vmem((2, 2 * H, FW), BF),
+        vmem((16, FW), BF),
+        vmem((FW, LANES), F32),
+        vmem((2, H, LANES), F32),
+        vmem((2, 8, LANES), F32),
+        vmem((mask_rows, KEY_TILE), F32),
+        vmem((3, EXT, S), BF),
+        vmem((5, 8, S), F32),
+        vmem((D, S), BF),
+        vmem((2, 2, H, T), F32),
+        vmem((2, 8, T), F32),
+        vmem((2, 8, T), F32),
+        vmem((2, 2, H, T), BF),
+        vmem((FW, S), BF),
+        vmem((FW, S), BF),
+        vmem((2, H, T), BF),
+        vmem((2, H, T), BF),
+        vmem((2, H, T), BF),
+        vmem((2, H, T), BF),
+        vmem((2, H, T), BF),
+        vmem((2, H, T), BF),
+        vmem((2, H, T), BF),
+        vmem((2, 2, H, T), BF),
+        vmem((H, T), BF),
+        vmem((H, T), BF),
+        vmem((H, T), BF),
+        vmem((EXT, S), BF),
+        vmem((3, EXT, S), BF),
+        vmem((HEAD_DIM, S), F32),
+        vmem((HEAD_DIM, S), F32),
+        vmem((2, 2 * H // 4, FW), BF),
+        vmem((4, 2, EXT, HP), BF),
+        vmem((2, R, HP), BF),
+        vmem((2, EXT - R, HP), BF),
+        vmem((H, T), F32),
+        vmem((H, LANES), F32),
+        vmem((2, 8, T), F32),
+        vmem((4, 8, FW), F32),
+        vmem((4, 2, 8, FW), F32),
+        vmem((8, FW), F32),
+        pltpu.SemaphoreType.DMA((SEND_COUNT,)),
+        pltpu.SemaphoreType.DMA((RECV_COUNT,)),
+        pltpu.SemaphoreType.DMA((LOCAL_COUNT,)),
+    ]
+    out_rows, in_rows, gf, gq, vectors, unused_rf, unused_rq = pl.pallas_call(
+        partial(layer_kernel, doc_count=doc_count),
+        out_shape=outs,
+        in_specs=[anywhere] * 8,
+        out_specs=[anywhere] * len(outs),
+        scratch_shapes=scratch,
+        compiler_params=pltpu.CompilerParams(
+            collective_id=0, has_side_effects=True, vmem_limit_bytes=VMEM_LIMIT
+        ),
+    )(tokens, cotangent, w3, out_weight, ff, fcb, vec, doc)
+    qkv_grad = jnp.transpose(gq[0:3, :, 0:H].astype(F32), (2, 0, 1))
+    bias_grad = jnp.stack([gq[0, :, H], gq[2, :, H]]).astype(F32)
+    return (
+        out_rows,
+        in_rows,
+        vectors[0, :H],
+        vectors[1, :H],
+        qkv_grad,
+        bias_grad,
+        gq[3, :, 0:H].astype(F32),
+        vectors[4, :H],
+        vectors[2, :H],
+        vectors[3, :H],
+        gf[0:H].astype(F32),
+        vectors[6],
+        gf[H:].astype(F32),
+        vectors[5, :H],
+    )
+
+
+def choose_body(*arrays):
+    sizes = {axis: lax.axis_size(axis) for axis in ("dp", "row", "col")}
+    H, R = arrays[0].shape[0], arrays[5].shape[0]
+    fits = sizes == {"dp": 4, "row": 4, "col": 2} and 4 * R == 2 * H == 17 * HEAD_DIM
+    return (fast_body if fits else body)(*arrays)
+
+
 def solution(mesh):
     return jax.shard_map(
-        body,
+        choose_body,
         mesh=mesh,
         in_specs=(
             P("col", ("dp", "row")),

time: 1640 us -> 314 us (0.19)
  waiting for transfers between devices: 890 us -> 0 us
  Pallas kernels: 0 us -> 281 us
  blocking collectives: 258 us -> 0 us
  local copies, waits for them, and re-layouts: 264 us -> 13.1 us
  matrix products: 113 us -> 0 us
  other arithmetic: 71.5 us -> 13.6 us
    reduce_scatter x9 -> x0, waiting for transfers between devices: 399 us -> none  [the longest x5 347 us: sum_over_rows(): lax.psum_scatter(row_term(jnp.int32(0), row_total * lax.axis_size('row'))...]
    all_gather x9 -> x0, waiting for transfers between devices: 308 us -> none  [the longest x4 185 us: gather_rows(): return lax.all_gather(values, 'row', axis=0, tiled=True)]
    pallas_call x0 -> x1, Pallas kernels: none -> 281 us  [fast_body(): pl.pallas_call(partial(layer_kernel, doc_count=doc_count), out_shape=outs...]
    dynamic_update_slice x4 -> x0, local copies, waits for them, and re-layouts: 177 us -> none  [attention_backward(): lax.scan(grad_step, jnp.zeros((query_count, head_count, head_width), jnp....]
    psum x1 -> x0, waiting for transfers between devices: 166 us -> none  [body(): lax.psum((qkv_weight_grad, qv_bias_grad, out_weight_grad, out_bias_grad,...]
    all_to_all x3 -> x0, blocking collectives: 150 us -> none  [the longest x1 76.8 us: to_heads(): lax.all_to_all(values, 'row', split_axis=0, concat_axis=2, tiled=True)]
    dot_general x30 -> x0, matrix products: 113 us -> none  [the longest x4 29.2 us: row_term(): return jnp.dot(full_rows, matrix, preferred_element_type=jnp.float32)]
    psum x6 -> x0, blocking collectives: 108 us -> none  [the longest x1 80.9 us: body(): lax.psum((ln1_gain_part, ln1_bias_part, ln2_gain_part, ln2_bias_part), ('...]
  transfers between devices with their start and end apart: 20 -> 0, of which waited for: 20 -> 0; matrix products, arithmetic and copies ran while one was open for 5% -> 0% of each run, Pallas kernels for 0% -> 0%
where the time goes in v1:
time: 314 us; the launch traced here: 308 us
  Pallas kernels  281 us (89%)
  other arithmetic  13.6 us (4%)
  local copies, waits for them, and re-layouts  13.1 us (4%)
    pallas_call x1, Pallas kernels, fast_body(): pl.pallas_call(partial(layer_kernel, doc_count=doc_count), out_shape=outs...  281 us

profile of v1, /device:TPU:0, one launch (start us, length us, event | category | flops | bytes accessed | tf_op | source)
XLA Modules:
  0.0 308.1 jit_solution(6799873544897651176)
XLA Ops:
  0.6 0.0 copy-start.1
  0.7 0.0 copy-start.2
  0.7 0.8 convert_element_type.27
  1.5 0.1 pad.23.clone
  1.6 0.7 broadcast_select_fusion
  2.2 0.1 pad.21.clone
  2.3 0.1 maximum_bitcast_fusion
  2.4 0.7 stack.34
  3.1 0.7 stack.35
  3.8 0.7 reshape.30
  4.5 0.7 stack.36
  5.2 0.7 stack.37
  5.9 0.7 reshape.31
  6.5 0.6 pad.14.doc_in
  7.1 0.7 broadcast_in_dim.15
  7.9 0.6 pad.12.fcb_in
  8.5 0.2 copy.36
  8.7 0.1 copy.37
  8.8 0.7 pad.13.vec_in
  9.6 2.5 maximum_maximum_fusion.w3_in
  12.1 0.0 copy-done.1
  12.1 0.0 copy-done.2
  12.1 1.7 pad_maximum_fusion.ff_in
  13.7 280.7 %shard_map.254 = (bf16[544,512]{1,0:T(8,128)(2,1)}, bf16[544,512]{1,0:T(8,128)(2,1)}, bf16[1088,1088]{1,0:T(8,128)(2,1)}, bf16[4,272,640]{2,1,0:T(8,128)(2,1)}, ...) custom-call(bf16[544,512]{1,0:T(8,128)(2,1)} %x_in.1, ...), custom_call_target="tpu_custom_call" | custom-call | tf_op jit(solution)/shard_map/pallas_call | solution.py:1288
  294.4 1.2 slice_reduce_fusion.1
  295.6 0.6 maximum_convert_fusion
  296.2 1.4 slice_reduce_fusion.2
  297.6 1.6 slice_reduce_fusion.3
  299.2 0.0 copy-start
  299.2 2.0 bitcast_convert_fusion
  301.2 2.7 convert_bitcast_fusion
  303.9 0.0 copy-done
  303.9 0.0 copy-start.4
  303.9 0.0 copy-start.3
  303.9 2.6 slice_convert_fusion
  306.5 0.0 copy-done.4
  306.5 0.8 copy.40
  307.3 0.0 copy-done.3
  307.3 0.8 copy.41
  (5 shorter events, 0.1 us)
Async XLA Ops:
  0.6 11.4 %copy-start.1 = (bf16[544,1088]{1,0:T(8,128)(2,1)S(1)}, bf16[544,1088]{1,0:T(8,128)(2,1)}, u32[]{:S(2)}) copy-start(bf16[544,1088]{1,0:T(8,128)(2,1)} %param.26) | copy-start | bytes 3551236
  0.7 11.4 %copy-start.2 = (bf16[544,1088]{1,0:T(8,128)(2,1)S(1)}, bf16[544,1088]{1,0:T(8,128)(2,1)}, u32[]{:S(2)}) copy-start(bf16[544,1088]{1,0:T(8,128)(2,1)} %param.24) | copy-start | bytes 3551236
  299.2 4.7 %copy-start = (bf16[1088,1088]{1,0:T(8,128)(2,1)S(1)}, bf16[1088,1088]{1,0:T(8,128)(2,1)}, u32[]{:S(2)}) copy-start(bf16[1088,1088]{1,0:T(8,128)(2,1)} %get-tuple-element.23) | copy-start | bytes 7102468
  303.9 2.6 copy-start.4
  303.9 3.4 %copy-start.3 = (bf16[544,512]{1,0:T(8,128)(2,1)S(1)}, bf16[544,512]{1,0:T(8,128)(2,1)}, u32[]{:S(2)}) copy-start(bf16[544,512]{1,0:T(8,128)(2,1)} %get-tuple-element.51) | copy-start | bytes 1671172

commit v2 on v1

--- a/solution.py
+++ b/solution.py
@@ -397,7 +397,7 @@
         return first
 
 
-SEND_COUNT, RECV_COUNT, LOCAL_COUNT = 112, 128, 32
+SEND_COUNT, RECV_COUNT, LOCAL_COUNT = 144, 160, 48
 
 
 def layer_kernel(
@@ -405,27 +405,27 @@
     cot_in,
     w3_in,
     ow_in,
-    ff_in,
-    fcb_in,
-    vec_in,
-    doc_in,
+    fc_in,
+    proj_in,
+    pack_in,
     out_o,
     ing_o,
     gf_o,
     gq_o,
     vec_o,
-    rf_hbm,
-    rq_hbm,
+    rf1_hbm,
+    rf2_hbm,
+    rq1_hbm,
+    rq2_hbm,
     XG,
     CG,
     N1,
     WB,
     OWB,
     FB,
-    FCB,
-    FCC,
-    VEC,
-    DOC,
+    COLS,
+    PACK,
+    PACKF,
     MASK,
     QKV,
     LSE,
@@ -476,7 +476,7 @@
     S = 2 * T
     W = KEY_TILE
     Q = HEAD_DIM
-    FW = ff_in.shape[1]
+    FW = fc_in.shape[1]
     per_tok = T // W
     n_tiles = S // W
     inv_d = 1.0 / D
@@ -494,6 +494,8 @@
     yn = lax.rem(dp + 2, 4)
     dg = 3 - dp
     peers = (dg, xn, yn)
+    xb, yb = lax.rem(dp, 2), dp // 2
+    xdev, ydev = (xn, z, c), (yn, z, c)
     first_core, second_core = c == 0, c == 1
 
     sends, recvs, locs = Slots(), Slots(), Slots()
@@ -550,24 +552,69 @@
 
     r_x_core, r_x_z, r_x_fwd = recvs.take(), recvs.take(), recvs.take()
     r_w_core, r_w_z, r_w_xy, r_w_tail = recvs.take(), recvs.take(2), recvs.take(4), recvs.take(2)
-    r_vec, r_doc = recvs.take(), recvs.take()
-
+    r_pack, r_packf = recvs.take(), recvs.take()
+    r_f_core, r_f_z, r_f_xy = recvs.take(2), recvs.take(2), recvs.take(4)
+    r_o_core, r_o_z, r_o_z0, r_o_xy, r_o_fwd = (
+        recvs.take(),
+        recvs.take(4),
+        recvs.take(4),
+        recvs.take(16),
+        recvs.take(4),
+    )
+
+    def block(number):
+        return pl.ds(pl.multiple_of(number * R, 16), R)
+
+    quarter = D // 4
+    odd = R - 4 * (R // 64) * 16
+    piece = R // 64 * 16
+
+    def quarter_rows(number):
+        return pl.ds(pl.multiple_of(number * quarter, 16), quarter)
+
+    def ow_piece(number, plane):
+        return pl.ds(pl.multiple_of(number * R + odd + plane * piece, 16), piece)
+
+    def ow_odd(number):
+        return pl.ds(pl.multiple_of(number * R, 16), odd)
+
+    my_quarter = quarter_rows(dp)
+    w_row = jnp.minimum(dp, 2)
+    has_before = z >= 1
+    push(w3_in.at[w_row], WB.at[w_row, c, pl.ds(0, R)], r_w_z + c, (dp, z2, 1), dp < 3)
     push(x_in, XG.at[zz, c], r_x_z, zdev)
-    w_row = jnp.minimum(dp, 2)
-    push(w3_in.at[w_row], WB.at[w_row, c, pl.ds(0, R)], r_w_z + c, (dp, z2, 1), dp < 3)
-    has_before = z >= 1
+    push(x_in, XG.at[zz, c], r_x_core, core)
+    push(pack_in, PACK.at[c], r_pack, core)
+    push(w3_in, WB.at[:, 1, pl.ds(0, R)], r_w_core, (dp, z, 0), second_core)
     push(w3_in.at[:, pl.ds(0, TAIL)], WB.at[:, c, pl.ds(R, TAIL)], r_w_tail + c, (dp, jnp.maximum(z - 1, 0), 0), has_before)
     push(w3_in.at[:, pl.ds(0, TAIL)], WB.at[:, c, pl.ds(R, TAIL)], r_w_tail + c, (dp, lax.rem(z + 1, 4), 1), has_before)
-    push(x_in, XG.at[zz, c], r_x_core, core)
-    push(w3_in, WB.at[:, 1, pl.ds(0, R)], r_w_core, (dp, z, 0), second_core)
-    push(doc_in, DOC.at[c], r_doc, core)
-    push(vec_in, VEC.at[c], r_vec, core)
+    push(pack_in, PACKF, r_packf, (dp, z2, 1), first_core)
     l_x = local(x_in, XG.at[zz, c])
+    l_pack = local(pack_in, PACK.at[c])
     l_w = local(w3_in, WB.at[:, 0, pl.ds(0, R)], first_core)
-    l_doc = local(doc_in, DOC.at[c])
-    l_vec = local(vec_in, VEC.at[c])
-
-    pad_rows = HP - H
+    push(
+        fc_in.at[quarter_rows(jnp.minimum(dp, 1))], FB.at[c, my_quarter], r_f_z + c, (dp, z2, 1), dp < 2
+    )
+    push(
+        proj_in.at[quarter_rows(jnp.maximum(dp - 2, 0))],
+        FB.at[c, my_quarter],
+        r_f_z + c,
+        (dp, z2, 1),
+        dp >= 2,
+    )
+    for step in (1, 3, 2):
+        target = (dp, lax.rem(z + step, 4), c)
+        push(ow_in.at[ow_piece(0, dp)], OWB.at[c, ow_piece(z, dp)], r_o_z + z, target)
+        push(ow_in.at[ow_odd(0)], OWB.at[c, ow_odd(z)], r_o_z0 + z, target)
+    push(fc_in, FB.at[1, pl.ds(0, H)], r_f_core, (dp, z, 0), second_core)
+    push(proj_in, FB.at[1, pl.ds(H, H)], r_f_core + 1, (dp, z, 0), second_core)
+    push(ow_in, OWB.at[c, block(z)], r_o_core, core)
+    l_f = local(fc_in, FB.at[0, pl.ds(0, H)], first_core)
+    l_p = local(proj_in, FB.at[0, pl.ds(H, H)], first_core)
+    l_o = local(ow_in, OWB.at[c, block(z)])
+
+    KD = N1.shape[2]
+    pad_rows = KD - H
     ones_row = (lax.broadcasted_iota(jnp.int32, (pad_rows, T), 0) == 0).astype(BF)
     for t in range(2):
         for h in range(2):
@@ -580,9 +627,9 @@
 
     pl.when(j == 3)(clear_tail)
 
-    done(l_doc)
-    arrived(DOC.at[oc], r_doc)
-    lengths = DOC[pair][0:1, :]
+    done(l_pack)
+    arrived(PACK.at[oc], r_pack)
+    lengths = PACK[pair, 7:8, 0:LANES]
     place_c = lax.broadcasted_iota(jnp.int32, (S, LANES), 0).astype(F32)
     place_r = lax.broadcasted_iota(jnp.int32, (8, S), 1).astype(F32)
     end = jnp.zeros((1, 1), F32)
@@ -602,11 +649,13 @@
         ok = (key_seg == seg_r[0:1, cols]) & (key_place <= place_r[0:1, cols])
         MASK[first : first + rows, :] = jnp.where(ok, 0.0, masked_fill)
 
-    done(l_vec)
-    arrived(VEC.at[oc], r_vec)
+    for h in range(2):
+        COLS[h * H : (h + 1) * H, 0:6] = PACK[h].T[0:H, 0:6]
 
     def column(h, which):
-        return VEC[h, :, which : which + 1]
+        if isinstance(h, int):
+            return COLS[h * H : (h + 1) * H, which : which + 1]
+        return COLS[pl.ds(pl.multiple_of(h * H, 16), H), which : which + 1]
 
     def stats_of(first_half, second_half):
         center = (
@@ -647,15 +696,6 @@
     arrived(XG.at[1 - zz, c], r_x_z)
     e_xf = push(XG.at[1 - zz, c], XG.at[1 - zz, c], r_x_fwd, core)
 
-    quarter = ff_in.shape[0] // 4
-    my_quarter = pl.ds(pl.multiple_of(dp * quarter, 16), quarter)
-    r_f_core, r_f_z, r_f_xy, r_fcb = recvs.take(), recvs.take(2), recvs.take(4), recvs.take()
-    push(ff_in.at[my_quarter], FB.at[c, my_quarter], r_f_z + c, (dp, z2, 1))
-    push(ff_in, FB.at[1], r_f_core, (dp, z, 0), second_core)
-    push(fcb_in, FCB, r_fcb, (dp, z2, 1), first_core)
-    l_f = local(ff_in, FB.at[0], first_core)
-    l_fcb = local(fcb_in, FCB, first_core)
-
     arrived(XG.at[1 - zz, oc], r_x_fwd)
     first_norm(1 - zz)
 
@@ -668,24 +708,28 @@
 
     for t in range(2):
         for m in range(3):
-            mixed = dot_nn(WB[m, 0], N1[t, 0]) + dot_nn(WB[m, 1], N1[t, 1])
+            mixed = dot_nn(WB[m, 0, :, 0:KD], N1[t, 0]) + dot_nn(WB[m, 1, :, 0:KD], N1[t, 1])
             low = mixed.astype(BF)
             if m == 0:
                 low = low * jnp.asarray(score_scale, BF)
             QKV[m, :, t * T : (t + 1) * T] = low
 
-    r_o_core, r_o_z, r_o_fwd = recvs.take(), recvs.take(4), recvs.take(4)
+    for h in range(2):
+        arrived(FB.at[h, my_quarter], r_f_z + h, second_core)
+    ff_entries = []
+    for peer in peers:
+        ff_entries.append(
+            push(FB.at[:, my_quarter], FB.at[:, my_quarter], r_f_xy + dp, (peer, z, 1), second_core)
+        )
+    for step in (1, 3, 2):
+        there = lax.rem(z + step, 4)
+        arrived(OWB.at[c, ow_piece(there, dp)], r_o_z + there)
+        for peer in peers:
+            rows = ow_piece(there, dp)
+            push(OWB.at[c, rows], OWB.at[c, rows], r_o_xy + (4 * dp + there), (peer, z, c))
     r_c_core, r_c_z, r_c_fwd = recvs.take(), recvs.take(), recvs.take()
-
-    def block(number):
-        return pl.ds(pl.multiple_of(number * R, 16), R)
-
-    for step in (1, 3, 2):
-        push(ow_in, OWB.at[c, block(z)], r_o_z + z, (dp, lax.rem(z + step, 4), c))
     push(cot_in, CG.at[zz, c], r_c_z, zdev)
-    push(ow_in, OWB.at[c, block(z)], r_o_core, core)
     push(cot_in, CG.at[zz, c], r_c_core, core)
-    l_o = local(ow_in, OWB.at[c, block(z)])
     l_c = local(cot_in, CG.at[zz, c])
 
     r_a_z, r_a_core, r_a_fwd = recvs.take(5), recvs.take(5), recvs.take(5)
@@ -701,19 +745,6 @@
     def att_copy(owner, slot, s_base, r_base, dev):
         rows = head_rows(owner, slot)
         return remote(ATT.at[rows], ATT.at[rows], s_base + slot, r_base + slot, dev)
-
-    forward_slot = 3
-    s_f_xy = sends.take(3)
-
-    def ff_copy(number):
-        part = FB.at[:, my_quarter]
-        return remote(part, part, s_f_xy + number, r_f_xy + dp, (peers[number], z, 1))
-
-    def forward_ff():
-        for h in range(2):
-            arrived(FB.at[h, my_quarter], r_f_z + h, second_core)
-        for number in range(3):
-            when(second_core, ff_copy(number).start)
 
     def attend(slot, carry):
         rows = slot_rows(slot)
@@ -735,10 +766,6 @@
         att_copy(j, slot, s_a_z, r_a_z, zdev).start()
         att_copy(j, slot, s_a_core, r_a_core, core).start()
 
-        @pl.when(slot == forward_slot)
-        def _():
-            forward_ff()
-
         return carry
 
     lax.fori_loop(first_slot, 5, attend, 0)
@@ -747,7 +774,9 @@
     push(CG.at[1 - zz, c], CG.at[1 - zz, c], r_c_fwd, core)
     for step in (1, 3, 2):
         there = lax.rem(z + step, 4)
-        arrived(OWB.at[c, block(there)], r_o_z + there)
+        arrived(OWB.at[c, ow_odd(there)], r_o_z0 + there)
+        for plane in range(4):
+            arrived(OWB.at[c, ow_piece(there, plane)], r_o_xy + (4 * plane + there), dp != plane)
         push(OWB.at[c, block(there)], OWB.at[c, block(there)], r_o_fwd + there, core)
 
     def owner_of(zv, cv):
@@ -792,18 +821,24 @@
     lax.fori_loop(0, n_tiles, project, 0)
 
     done(l_f)
-    done(l_fcb)
-    arrived(FB.at[1], r_f_core, first_core)
-    arrived(FCB, r_fcb, second_core)
+    done(l_p)
+    for number in range(2):
+        arrived(FB.at[1, pl.ds(number * H, H)], r_f_core + number, first_core)
     for number in range(4):
-        rows = pl.ds(number * quarter, quarter)
-        arrived(FB.at[:, rows], r_f_xy + number, second_core & (dp != number))
+        arrived(FB.at[:, quarter_rows(number)], r_f_xy + number, second_core & (dp != number))
+    arrived(PACKF, r_packf, second_core)
+
+    @pl.when(first_core)
+    def _():
+        COLS[:, 6:7] = PACK[0].T[0:FW, 6:7]
+
+    @pl.when(second_core)
+    def _():
+        COLS[:, 6:7] = PACKF[...].T[0:FW, 6:7]
+
     done(l_c)
     arrived(CG.at[zz, oc], r_c_core)
     arrived(CG.at[1 - zz, oc], r_c_fwd)
-
-    one_row = (lax.broadcasted_iota(jnp.int32, (16, LANES), 0) == 0).astype(BF)
-    FCC[...] = dot_tn(FCB[...], one_row)
 
     r_g_core, r_p_core, r_g_z = recvs.take(n_tiles), recvs.take(n_tiles), recvs.take(n_tiles)
     s_g_core, s_p_core, s_g_z = sends.take(n_tiles), sends.take(n_tiles), sends.take(n_tiles)
@@ -822,7 +857,7 @@
         pre = (
             dot_tn(FB[0, 0:H], N2[t, 0, :, cols])
             + dot_tn(FB[1, 0:H], N2[t, 1, :, cols])
-            + FCC[:, 0:1]
+            + COLS[:, 6:7]
         )
         phi = 0.5 * (1.0 + lax.erf(pre * (2.0**-0.5)))
         ACT[:, all_cols] = (pre * phi).astype(BF)
@@ -832,37 +867,19 @@
         PGS[t, :, cols] = dot_nn(FB[oc, 0:H], GPRE[:, all_cols]).astype(BF)
         part_copy(PGS, RCG, tile, s_g_core, r_g_core, core).start()
         own = dot_nn(FB[c, 0:H], GPRE[:, all_cols])
-        OPS[t, :, cols] = dot_nn(FB[oc, H:D], ACT[:, all_cols]).astype(BF)
-        part_copy(OPS, RCO, tile, s_p_core, r_p_core, core).start()
         part_copy(PGS, RCG, tile, s_g_core, r_g_core, core).wait_recv()
         SZG[t, :, cols] = (own + RCG[t, :, cols].astype(F32)).astype(BF)
         part_copy(SZG, RZG, tile, s_g_z, r_g_z, zdev).start()
-        OPO[t, :, cols] = dot_nn(FB[c, H:D], ACT[:, all_cols]).astype(BF)
         return carry
 
     lax.fori_loop(0, n_tiles, feed, 0)
 
-    def wait_sends(tile, carry):
-        part_copy(PGS, RCG, tile, s_g_core, r_g_core, core).wait_send()
-        part_copy(OPS, RCO, tile, s_p_core, r_p_core, core).wait_send()
-        return carry
-
-    r_out_z = recvs.take()
-
-    def wait_out(tile, carry):
-        part_copy(OPS, RCO, tile, s_p_core, r_p_core, core).wait_recv()
-        return carry
-
-    lax.fori_loop(0, n_tiles, wait_out, 0)
-    SZO[...] = (OPO[1 - zz].astype(F32) + RCO[1 - zz].astype(F32)).astype(BF)
-    push(SZO, RZO, r_out_z, zdev)
-
-    for number in range(3):
-        when(second_core, ff_copy(number).wait_send)
-    r_rf = recvs.take(4)
-    rf_entries = []
-    for number in range(4):
-        rows = slice(number * quarter, (number + 1) * quarter)
+    for entry in ff_entries:
+        sent(entry)
+    r_f1, r_f2 = recvs.take(4), recvs.take(2)
+    f1_entries = []
+
+    def ff_grads(number):
         for h in range(2):
             if number < 2:
                 left, right, low = N2, GPRE, number * quarter
@@ -871,16 +888,35 @@
             total = dot_nt(left[0, h, low : low + quarter, :], right[:, 0:T]) + dot_nt(
                 left[1, h, low : low + quarter, :], right[:, T:S]
             )
-            FB[h, rows, :] = total.astype(BF)
-        rf_entries.append(
-            push(
-                FB.at[:, pl.ds(number * quarter, quarter)],
-                rf_hbm.at[dp],
-                r_rf + dp,
-                (number, z, c),
-                dp != number,
-            )
-        )
+            FB[h, number * quarter : (number + 1) * quarter, :] = total.astype(BF)
+
+    def ff_part(h, number):
+        return FB.at[h, quarter_rows(number)]
+
+    def f1_push(h, number, place, dev, cond=None):
+        f1_entries.append(push(ff_part(h, number), rf1_hbm.at[place], r_f1 + place, dev, cond))
+
+    ff_grads(0)
+    ff_grads(1)
+    f1_push(0, 1 - xb, 0, xdev)
+    for number in range(2):
+        f1_push(1, number, 2 + number, ydev, yb == 1)
+
+    def outward(tile, carry):
+        t, cols = tile_at(tile)
+        all_cols = pl.ds(pl.multiple_of(tile * W, W), W)
+        OPS[t, :, cols] = dot_nn(FB[oc, H:D], ACT[:, all_cols]).astype(BF)
+        part_copy(OPS, RCO, tile, s_p_core, r_p_core, core).start()
+        OPO[t, :, cols] = dot_nn(FB[c, H:D], ACT[:, all_cols]).astype(BF)
+        return carry
+
+    lax.fori_loop(0, n_tiles, outward, 0)
+    ff_grads(2)
+    ff_grads(3)
+    f1_push(0, 3 - xb, 1, xdev)
+    for number in range(2):
+        f1_push(1, 2 + number, 2 + number, ydev, yb == 0)
+
     SPR[dp] = jnp.zeros(SPR.shape[1:], F32)
     SPR[dp, 6:7, :] = dot_nt(jnp.ones((16, S), BF), GPRE[...])[0:1, :]
 
@@ -932,6 +968,16 @@
     sent(e_xf)
     lax.fori_loop(0, n_tiles, second_back, 0)
     GB = XG
+
+    r_out_z = recvs.take()
+
+    def wait_out(tile, carry):
+        part_copy(OPS, RCO, tile, s_p_core, r_p_core, core).wait_recv()
+        return carry
+
+    lax.fori_loop(0, n_tiles, wait_out, 0)
+    SZO[...] = (OPO[1 - zz].astype(F32) + RCO[1 - zz].astype(F32)).astype(BF)
+    push(SZO, RZO, r_out_z, zdev)
     VGC[:, 4:5] = jnp.sum(GB[zz, c].astype(F32), axis=1, keepdims=True)
     VGC[:, 5:6] = jnp.sum(CG[zz, c].astype(F32), axis=1, keepdims=True)
 
@@ -940,13 +986,52 @@
         DATT[:, t * T : (t + 1) * T] = (
             dot_nn(OWB[0, window, :], GB[t, 0]) + dot_nn(OWB[1, window, :], GB[t, 1])
         ).astype(BF)
-    r_rq = recvs.take(4)
-    rq_entries = []
+    r_q1, r_q2 = recvs.take(4), recvs.take(2)
+    q1_entries = []
+
+    def q1_push(h, number, place, dev, cond=None):
+        q1_entries.append(push(DQ.at[number, h], rq1_hbm.at[place], r_q1 + place, dev, cond))
+
     for h in range(2):
         total = dot_nt(ATT[block(j), 0:T], GB[0, h]) + dot_nt(ATT[block(j), T:S], GB[1, h])
         DQ[3, h, 0:R, 0:H] = total.astype(BF)
-    rq_entries.append(push(DQ.at[3], rq_hbm.at[dp], r_rq + dp, (3, z, c), dp != 3))
+    q1_push(0, 3, 1, xdev, xb == 0)
+    q1_push(1, 3, 3, ydev, yb == 0)
     l_x2 = local(x_in, XG.at[zz, c])
+
+    s_f2 = sends.take(2)
+    l_f1, l_f2 = locs.take(4), locs.take(2)
+
+    def f2_copy(place):
+        if place == 0:
+            return remote(ff_part(0, xb + 2 * (1 - yb)), rf2_hbm.at[0], s_f2, r_f2, ydev)
+        return remote(ff_part(1, 2 * yb + 1 - xb), rf2_hbm.at[1], s_f2 + 1, r_f2 + 1, xdev)
+
+    spare = ((0, 1 - xb), (0, 3 - xb), (1, 2 * (1 - yb)), (1, 2 * (1 - yb) + 1))
+    kept = ((0, xb), (0, 2 + xb), (1, 2 * yb), (1, 2 * yb + 1))
+
+    def first_join():
+        for entry in f1_entries:
+            when(entry[0], entry[1].wait_send)
+        loads = []
+        for place in range(4):
+            arrived(rf1_hbm.at[place], r_f1 + place)
+            load = pltpu.make_async_copy(rf1_hbm.at[place], ff_part(*spare[place]), LS.at[l_f1 + place])
+            load.start()
+            loads.append(load)
+        for load in loads:
+            load.wait()
+
+        def add(place):
+            h, number = kept[place]
+            other = FB[spare[place][0], quarter_rows(spare[place][1]), :]
+            rows = quarter_rows(number)
+            FB[h, rows, :] = (FB[h, rows, :].astype(F32) + other.astype(F32)).astype(BF)
+
+        for place in range(4):
+            add(place)
+        f2_copy(0).start()
+        f2_copy(1).start()
 
     def attend_back(slot, carry):
         rows = slot_rows(slot)
@@ -977,6 +1062,11 @@
             GQKV[0, rows, cols] = (dot_nn(keys_t[:, :count], grad_scores) * score_scale).astype(BF)
         GQKV[1, rows, :] = ACCK[...].astype(BF)
         GQKV[2, rows, :] = ACCV[...].astype(BF)
+
+        @pl.when(slot == 3)
+        def _():
+            first_join()
+
         return carry
 
     lax.fori_loop(first_slot, 5, attend_back, 0)
@@ -984,8 +1074,9 @@
     for m in range(3):
         for h in range(2):
             total = dot_nt(GQKV[m, :, 0:T], N1[0, h]) + dot_nt(GQKV[m, :, T:S], N1[1, h])
-            DQ[m, h] = total.astype(BF)
-        rq_entries.append(push(DQ.at[m], rq_hbm.at[dp], r_rq + dp, (m, z, c), dp != m))
+            DQ[m, h, :, 0:KD] = total.astype(BF)
+        q1_push(0, m, m // 2, xdev, xb != m % 2)
+        q1_push(1, m, 2 + m % 2, ydev, yb != m // 2)
 
     def wait_sends(tile, carry):
         part_copy(PGS, RCG, tile, s_g_core, r_g_core, core).wait_send()
@@ -1022,39 +1113,48 @@
     SZG[0] = (OPS[1 - zz].astype(F32) + RCG[1 - zz].astype(F32)).astype(BF)
     push(SZG.at[0], RZN, r_n_z, zdev)
 
-    for entry in rf_entries:
-        sent(entry)
+    for entry in f1_entries:
+        pending[:] = [other for other in pending if other is not entry]
     loads = []
-    for number in range(4):
-        other = dp != number
-        arrived(rf_hbm.at[number], r_rf + number, other)
-        loads.append(
-            local(rf_hbm.at[number], FB.at[:, pl.ds(number * quarter, quarter)], other)
-        )
-    for entry in loads:
-        done(entry)
+    for h in range(2):
+        arrived(rf2_hbm.at[h], r_f2 + h)
+        loads.append(local(rf2_hbm.at[h], ff_part(*spare[2 * h])))
     r_zf = recvs.take(2)
-    first_rows = slice(0, quarter)
     for h in range(2):
-        total = FB[h, 0:quarter, :].astype(F32)
-        for number in range(1, 4):
-            total = total + FB[h, number * quarter : (number + 1) * quarter, :].astype(F32)
-        low = total.astype(BF)
-        FB[h, 0:quarter, :] = low
+        done(loads[h])
+        low = (
+            FB[h, my_quarter, :].astype(F32) + FB[h, quarter_rows(spare[2 * h][1]), :].astype(F32)
+        ).astype(BF)
+        FB[h, my_quarter, :] = low
         if h == 0:
 
             @pl.when(first_core)
             def _():
                 ZF[0] = low
 
-        push(FB.at[h, pl.ds(0, quarter)], ZF.at[1], r_zf + 1, (dp, z2, h), second_core)
+        push(FB.at[h, my_quarter], ZF.at[1], r_zf + 1, (dp, z2, h), second_core)
         if h == 1:
-            push(FB.at[h, pl.ds(0, quarter)], ZF.at[0], r_zf, (dp, z, 1), first_core)
+            push(FB.at[h, my_quarter], ZF.at[0], r_zf, (dp, z, 1), first_core)
 
     arrived(RZO, r_out_z)
     branch_out = OPO[zz].astype(F32) + RCO[zz].astype(F32) + RZO[...].astype(F32)
-    OPO[0] = (HID[zz, c] + branch_out + VEC[c, :, VEC_PROJ_BIAS : VEC_PROJ_BIAS + 1]).astype(BF)
+    OPO[0] = (HID[zz, c] + branch_out + column(c, VEC_PROJ_BIAS)).astype(BF)
     l_out = local(OPO.at[0], out_o)
+
+    for entry in q1_entries:
+        sent(entry)
+    q_spare = ((1 - xb, 0), (3 - xb, 0), (2 * (1 - yb), 1), (2 * (1 - yb) + 1, 1))
+    q_kept = ((xb, 0), (2 + xb, 0), (2 * yb, 1), (2 * yb + 1, 1))
+    loads = []
+    for place in range(4):
+        arrived(rq1_hbm.at[place], r_q1 + place)
+        loads.append(local(rq1_hbm.at[place], DQ.at[q_spare[place][0], q_spare[place][1]]))
+    for place in range(4):
+        done(loads[place])
+        (there, h), (here, unused) = q_spare[place], q_kept[place]
+        DQ[here, h] = (DQ[here, h].astype(F32) + DQ[there, h].astype(F32)).astype(BF)
+    push(DQ.at[xb + 2 * (1 - yb), 0], rq2_hbm.at[0], r_q2, ydev)
+    push(DQ.at[2 * yb + 1 - xb, 1], rq2_hbm.at[1], r_q2 + 1, xdev)
 
     done(l_x2)
     arrived(RZN, r_n_z)
@@ -1062,7 +1162,7 @@
     grads = OPS[zz].astype(F32) + RCG[zz].astype(F32) + RZN[...].astype(F32)
     center, inv_std = ST1[zz, 0:1, :], ST1[zz, 1:2, :]
     normals = (XG[zz, c].astype(F32) - center) * inv_std
-    scaled = grads * VEC[c, :, VEC_LN1_GAIN : VEC_LN1_GAIN + 1]
+    scaled = grads * column(c, VEC_LN1_GAIN)
     STX[c, 0:1, :] = jnp.sum(scaled, axis=0, keepdims=True)
     STX[c, 1:2, :] = jnp.sum(scaled * normals, axis=0, keepdims=True)
     push(STX.at[c], STX.at[c], r_stat, core)
@@ -1079,35 +1179,6 @@
     for peer in peers:
         push(SPR.at[dp], SPR.at[dp], r_sp + dp, (peer, z, c))
 
-    for entry in rq_entries:
-        sent(entry)
-    loads = []
-    for number in range(4):
-        other = dp != number
-        arrived(rq_hbm.at[number], r_rq + number, other)
-        loads.append(local(rq_hbm.at[number], DQ.at[number], other))
-    for entry in loads:
-        done(entry)
-    r_zq, r_zt = recvs.take(2), recvs.take(2)
-    with_tail = (j < 3) & (dp < 3)
-    next_block = jnp.minimum(j + 1, 3)
-    for h in range(2):
-        total = DQ[0, h].astype(F32)
-        for number in range(1, 4):
-            total = total + DQ[number, h].astype(F32)
-        low = total.astype(BF)
-        DQ[0, h] = low
-        if h == 0:
-
-            @pl.when(first_core)
-            def _():
-                ZQ[0] = low[0:R]
-
-        push(DQ.at[0, h, pl.ds(0, R)], ZQ.at[1], r_zq + 1, (dp, z2, h), second_core)
-        if h == 1:
-            push(DQ.at[0, h, pl.ds(0, R)], ZQ.at[0], r_zq, (dp, z, 1), first_core)
-        push(DQ.at[0, h, pl.ds(R, TAIL)], ZT.at[c], r_zt + c, (dp, next_block, h), with_tail)
-
     r_gf, r_gq = recvs.take(4), recvs.take(4)
     arrived(ZF.at[0], r_zf, second_core)
     arrived(ZF.at[1], r_zf + 1)
@@ -1115,6 +1186,28 @@
     l_gf = local(ZF.at[0], gf_o.at[my_quarter])
     for peer in peers:
         push(ZF.at[0], gf_o.at[my_quarter], r_gf + dp, (peer, z, c))
+
+    loads = []
+    for h in range(2):
+        arrived(rq2_hbm.at[h], r_q2 + h)
+        loads.append(local(rq2_hbm.at[h], DQ.at[q_spare[2 * h][0], h]))
+    r_zq, r_zt = recvs.take(2), recvs.take(2)
+    with_tail = (j < 3) & (dp < 3)
+    next_block = jnp.minimum(j + 1, 3)
+    for h in range(2):
+        done(loads[h])
+        low = (DQ[dp, h].astype(F32) + DQ[q_spare[2 * h][0], h].astype(F32)).astype(BF)
+        DQ[dp, h] = low
+        if h == 0:
+
+            @pl.when(first_core)
+            def _():
+                ZQ[0] = low[0:R]
+
+        push(DQ.at[dp, h, pl.ds(0, R)], ZQ.at[1], r_zq + 1, (dp, z2, h), second_core)
+        if h == 1:
+            push(DQ.at[dp, h, pl.ds(0, R)], ZQ.at[0], r_zq, (dp, z, 1), first_core)
+        push(DQ.at[dp, h, pl.ds(R, TAIL)], ZT.at[c], r_zt + c, (dp, next_block, h), with_tail)
 
     for number in range(4):
         arrived(SPR.at[number], r_sp + number, dp != number)
@@ -1169,6 +1262,9 @@
         lambda slot: att_copy(owner_of(zp, c), slot, s_a_fwd, r_a_fwd, core).wait_send(),
     )
 
+    f2_copy(0).wait_send()
+    f2_copy(1).wait_send()
+
     def last_sends(tile, carry):
         part_copy(PGS, RCG, tile, s_n_core, r_n_core, core).wait_send()
         return carry
@@ -1177,6 +1273,75 @@
     for entry in list(pending):
         sent(entry)
     assert sends.used <= SEND_COUNT and recvs.used <= RECV_COUNT and locs.used <= LOCAL_COUNT
+
+
+def finish_kernel(
+    out_in,
+    ing_in,
+    gf_in,
+    gq_in,
+    vec_in,
+    out_o,
+    ing_o,
+    qkv_o,
+    qvb_o,
+    ow_o,
+    fc_o,
+    proj_o,
+    v0,
+    v1,
+    v2,
+    v3,
+    v4,
+    v5,
+    v6,
+    GF,
+    GQ,
+    FST,
+    QST,
+    SEM,
+):
+    R, H = ow_o.shape
+    count = GF.shape[0] // R
+    whole = [
+        pltpu.make_async_copy(out_in, out_o, SEM.at[0]),
+        pltpu.make_async_copy(ing_in, ing_o, SEM.at[1]),
+    ]
+    place = 2
+    loads_q, loads_f = [], []
+    for m in range(4):
+        loads_q.append(pltpu.make_async_copy(gq_in.at[m], GQ.at[m], SEM.at[place + m]))
+    place += 4
+    for number in range(count):
+        rows = pl.ds(number * R, R)
+        loads_f.append(pltpu.make_async_copy(gf_in.at[rows], GF.at[rows], SEM.at[place + number]))
+    place += count
+    for copy in loads_f + loads_q + whole:
+        copy.start()
+    stores = []
+    for number in range(count):
+        loads_f[number].wait()
+        rows = pl.ds(number * R, R)
+        FST[rows, :] = GF[rows, :].astype(F32)
+        half = count // 2
+        dst = (fc_o if number < half else proj_o).at[pl.ds(number % half * R, R)]
+        stores.append(pltpu.make_async_copy(FST.at[rows], dst, SEM.at[place + number]))
+        stores[-1].start()
+    place += count
+    for m in range(4):
+        loads_q[m].wait()
+        QST[m] = GQ[m, :, 0:H].astype(F32)
+        dst = qkv_o.at[m] if m < 3 else ow_o
+        stores.append(pltpu.make_async_copy(QST.at[m], dst, SEM.at[place + m]))
+        stores[-1].start()
+    first = H // LANES * LANES
+    for number, m in enumerate((0, 2)):
+        turned = GQ[m, :, first : first + LANES].astype(F32).T
+        qvb_o[number : number + 1, :] = turned[H - first : H - first + 1, :]
+    for number, v in enumerate((v0, v1, v2, v3, v4, v5, v6)):
+        v[...] = vec_in[number, 0 : v.shape[0]]
+    for copy in stores + whole:
+        copy.wait()
 
 
 def fast_body(
@@ -1215,13 +1380,11 @@
         ],
         axis=2,
     )
-    ff = jnp.concatenate([fc_weight, proj_weight], axis=0)
-    fcb = jnp.pad(fc_bias[None], ((0, 15), (0, 0)))
-    vec = jnp.stack(
-        [ln1_gain, ln1_bias, ln2_gain, ln2_bias, out_bias.astype(F32), proj_bias.astype(F32)], axis=1
-    )
-    vec = jnp.pad(vec, ((0, 0), (0, LANES - 6)))
-    doc = jnp.pad(doc_lengths.astype(F32), ((0, 7), (0, LANES - doc_count)))
+    rows = [ln1_gain, ln1_bias, ln2_gain, ln2_bias, out_bias, proj_bias, fc_bias, doc_lengths[0]]
+    wide = (FW // LANES + 1) * LANES
+    pack = jnp.concatenate(
+        [jnp.pad(row.astype(F32)[None], ((0, 0), (0, wide - row.shape[0]))) for row in rows], axis=0
+    )
     shape = jax.ShapeDtypeStruct
     anywhere = pl.BlockSpec(memory_space=pl.ANY)
     outs = [
@@ -1230,22 +1393,23 @@
         shape((2 * H, FW), BF),
         shape((4, R, HP), BF),
         shape((8, FW), F32),
-        shape((4, 2, 2 * H // 4, FW), BF),
-        shape((4, 2, EXT, HP), BF),
+        shape((4, D // 4, FW), BF),
+        shape((2, D // 4, FW), BF),
+        shape((4, EXT, HP), BF),
+        shape((2, EXT, HP), BF),
     ]
     vmem = pltpu.VMEM
     mask_rows = KEY_TILE * NT * (NT + 1) // 2
     scratch = [
         vmem((2, 2, H, T), BF),
         vmem((2, 2, H, T), BF),
-        vmem((2, 2, HP, T), BF),
+        vmem((2, 2, H + 16, T), BF),
         vmem((3, 2, EXT, HP), BF),
         vmem((2, D, H), BF),
         vmem((2, 2 * H, FW), BF),
-        vmem((16, FW), BF),
         vmem((FW, LANES), F32),
-        vmem((2, H, LANES), F32),
-        vmem((2, 8, LANES), F32),
+        vmem((2, 8, wide), F32),
+        vmem((8, wide), F32),
         vmem((mask_rows, KEY_TILE), F32),
         vmem((3, EXT, S), BF),
         vmem((5, 8, S), F32),
@@ -1285,33 +1449,58 @@
         pltpu.SemaphoreType.DMA((RECV_COUNT,)),
         pltpu.SemaphoreType.DMA((LOCAL_COUNT,)),
     ]
-    out_rows, in_rows, gf, gq, vectors, unused_rf, unused_rq = pl.pallas_call(
+    out_rows, in_rows, gf, gq, vectors = pl.pallas_call(
         partial(layer_kernel, doc_count=doc_count),
         out_shape=outs,
-        in_specs=[anywhere] * 8,
+        in_specs=[anywhere] * 7,
         out_specs=[anywhere] * len(outs),
         scratch_shapes=scratch,
         compiler_params=pltpu.CompilerParams(
             collective_id=0, has_side_effects=True, vmem_limit_bytes=VMEM_LIMIT
         ),
-    )(tokens, cotangent, w3, out_weight, ff, fcb, vec, doc)
-    qkv_grad = jnp.transpose(gq[0:3, :, 0:H].astype(F32), (2, 0, 1))
-    bias_grad = jnp.stack([gq[0, :, H], gq[2, :, H]]).astype(F32)
+    )(tokens, cotangent, w3, out_weight, fc_weight, proj_weight, pack)[:5]
+    in_vmem = pl.BlockSpec(memory_space=vmem)
+    finals = pl.pallas_call(
+        finish_kernel,
+        out_shape=[
+            shape((H, T), BF),
+            shape((H, T), BF),
+            shape((3, R, H), F32),
+            shape((2, R), F32),
+            shape((R, H), F32),
+            shape((H, FW), F32),
+            shape((H, FW), F32),
+        ]
+        + [shape((H,), F32)] * 6
+        + [shape((FW,), F32)],
+        in_specs=[anywhere] * 4 + [in_vmem],
+        out_specs=[anywhere] * 3 + [in_vmem] + [anywhere] * 3 + [in_vmem] * 7,
+        scratch_shapes=[
+            vmem((D, FW), BF),
+            vmem((4, R, HP), BF),
+            vmem((D, FW), F32),
+            vmem((4, R, H), F32),
+            pltpu.SemaphoreType.DMA((32,)),
+        ],
+        compiler_params=pltpu.CompilerParams(vmem_limit_bytes=32_000_000),
+    )(out_rows, in_rows, gf, gq, vectors)
+    out_final, in_final, qkv_rows, bias_grad, ow_grad, fc_grad, proj_grad = finals[:7]
+    ln1_gain_g, ln1_bias_g, ln2_gain_g, ln2_bias_g, out_bias_g, proj_bias_g, fc_bias_g = finals[7:]
     return (
-        out_rows,
-        in_rows,
-        vectors[0, :H],
-        vectors[1, :H],
-        qkv_grad,
+        out_final,
+        in_final,
+        ln1_gain_g,
+        ln1_bias_g,
+        jnp.transpose(qkv_rows, (2, 0, 1)),
         bias_grad,
-        gq[3, :, 0:H].astype(F32),
-        vectors[4, :H],
-        vectors[2, :H],
-        vectors[3, :H],
-        gf[0:H].astype(F32),
-        vectors[6],
-        gf[H:].astype(F32),
-        vectors[5, :H],
+        ow_grad,
+        out_bias_g,
+        ln2_gain_g,
+        ln2_bias_g,
+        fc_grad,
+        fc_bias_g,
+        proj_grad,
+        proj_bias_g,
     )
 
 

time: 314 us -> 282 us (0.90); the launches traced: 308 us -> 281 us
  Pallas kernels: 281 us -> 264 us
  other arithmetic: 13.6 us -> 3.92 us
    pallas_call x1, Pallas kernels: 281 us -> 259 us  [fast_body(): pl.pallas_call(partial(layer_kernel, doc_count=doc_count), out_shape=outs...]
    pallas_call x0 -> x1, Pallas kernels: none -> 5.66 us  [fast_body(): pl.pallas_call(finish_kernel, out_shape=[shape((H, T), BF), shape((H, T),...]
    convert_element_type x4 -> x1, other arithmetic: 6.02 us -> 0.66 us  [fast_body(): row.astype(F32)[None]]
    another operation x10 -> x0, local copies, waits for them, and re-layouts: 4.32 us -> none  [the longest x8 4.31 us: fast_body(): jnp.stack([ln1_gain, ln1_bias, ln2_gain, ln2_bias, out_bias.astype(F32),...]
    unnamed x12 -> x10, local copies, waits for them, and re-layouts: 1.63 us -> 5.92 us
    slice x3 -> x0, local copies, waits for them, and re-layouts: 4.14 us -> none  [the longest x1 1.6 us: fast_body(): vectors[5, :H]]
    broadcast_in_dim x1 -> x7, local copies, waits for them, and re-layouts: 0.69 us -> 4.82 us  [fast_body(): row.astype(F32)[None]]
where the time goes in v2:
time: 282 us; the launch traced here: 281 us
  Pallas kernels  264 us (94%)
  local copies, waits for them, and re-layouts  11.8 us (4%)
  other arithmetic  3.92 us (1%)
    pallas_call x1, Pallas kernels, fast_body(): pl.pallas_call(partial(layer_kernel, doc_count=doc_count), out_shape=outs...  259 us
    unnamed x10, local copies, waits for them, and re-layouts  5.92 us
    pallas_call x1, Pallas kernels, fast_body(): pl.pallas_call(finish_kernel, out_shape=[shape((H, T), BF), shape((H, T),...  5.66 us

profile of v2, /device:TPU:0, one launch (start us, length us, event | category | flops | bytes accessed | tf_op | source)
XLA Modules:
  0.0 281.0 jit_solution(4786955251650513004)
XLA Ops:
  0.6 0.7 convert_element_type.18
  1.3 0.1 pad.51.clone
  1.4 0.7 broadcast_select_fusion
  2.1 0.1 pad.49.clone
  2.2 0.1 maximum_bitcast_fusion
  2.2 0.7 broadcast_in_dim.37
  2.9 0.7 broadcast_in_dim.38
  3.6 0.7 broadcast_in_dim.41
  4.3 0.7 broadcast_in_dim.39
  5.0 0.7 broadcast_in_dim.40
  5.7 0.7 broadcast_in_dim.42
  6.4 0.7 broadcast_in_dim.43
  7.1 0.7 concatenate.7.pack_in
  7.8 0.2 copy.29
  8.0 2.5 maximum_maximum_fusion.w3_in
  10.5 258.7 %shard_map.254 = (bf16[544,512]{1,0:T(8,128)(2,1)}, bf16[544,512]{1,0:T(8,128)(2,1)}, bf16[1088,1088]{1,0:T(8,128)(2,1)}, bf16[4,272,640]{2,1,0:T(8,128)(2,1)}, ...) custom-call(bf16[544,512]{1,0:T(8,128)(2,1)} %x_in.1, ...), custom_call_target="tpu_custom_call" | custom-call | tf_op jit(solution)/shard_map/pallas_call | solution.py:1452
  269.2 0.0 copy-start
  269.2 1.7 copy-done
  270.9 0.0 copy-start.1
  270.9 1.3 copy-done.1
  272.3 0.0 copy-start.2
  272.3 1.1 copy-done.2
  273.3 0.0 copy-start.3
  273.3 1.1 copy-done.3
  274.4 0.0 copy-start.4
  274.4 0.8 copy-done.4
  275.2 5.7 %shard_map.255 = (bf16[544,512]{1,0:T(8,128)(2,1)}, bf16[544,512]{1,0:T(8,128)(2,1)}, f32[3,272,544]{2,1,0:T(8,128)}, f32[2,272]{1,0:T(2,128)}, f32[272,544]{1,0...) custom-call(bf16[544,512]{1,0:T(8,128)(2,1)S(1)} %copy-done.2, ...), custom_call_target="tpu_custom_call" | custom-call | tf_op jit(solution)/shard_map/pallas_call | solution.py:1463
  (9 shorter events, 0.1 us)
Async XLA Ops:
  269.2 1.7 copy-start
  270.9 1.3 copy-start.1
  272.3 1.1 copy-start.2
  273.3 1.1 copy-start.3
  274.4 0.8 copy-start.4

commit v3 on v2

--- a/solution.py
+++ b/solution.py
@@ -407,7 +407,15 @@
     ow_in,
     fc_in,
     proj_in,
-    pack_in,
+    ln1_gain_in,
+    ln1_bias_in,
+    ln2_gain_in,
+    ln2_bias_in,
+    out_bias_in,
+    proj_bias_in,
+    fc_bias_in,
+    qv_bias_in,
+    doc_in,
     out_o,
     ing_o,
     gf_o,
@@ -421,11 +429,13 @@
     CG,
     N1,
     WB,
+    QB,
     OWB,
     FB,
     COLS,
     PACK,
     PACKF,
+    PACKN,
     MASK,
     QKV,
     LSE,
@@ -464,12 +474,10 @@
     SS,
     RS,
     LS,
-    *,
-    doc_count,
 ):
     H, T = x_in.shape
     R = w3_in.shape[1]
-    HP = w3_in.shape[2]
+    HP = DQ.shape[3]
     EXT = WB.shape[2]
     TAIL = EXT - R
     D = 2 * H
@@ -552,7 +560,7 @@
 
     r_x_core, r_x_z, r_x_fwd = recvs.take(), recvs.take(), recvs.take()
     r_w_core, r_w_z, r_w_xy, r_w_tail = recvs.take(), recvs.take(2), recvs.take(4), recvs.take(2)
-    r_pack, r_packf = recvs.take(), recvs.take()
+    r_pack, r_packf, r_packn = recvs.take(), recvs.take(), recvs.take()
     r_f_core, r_f_z, r_f_xy = recvs.take(2), recvs.take(2), recvs.take(4)
     r_o_core, r_o_z, r_o_z0, r_o_xy, r_o_fwd = (
         recvs.take(),
@@ -581,31 +589,28 @@
     my_quarter = quarter_rows(dp)
     w_row = jnp.minimum(dp, 2)
     has_before = z >= 1
+    bias_first = (LANES, LANES + (R // LANES + 1) * LANES)
+    doc_count = doc_in.shape[1]
     push(w3_in.at[w_row], WB.at[w_row, c, pl.ds(0, R)], r_w_z + c, (dp, z2, 1), dp < 3)
+    pack = PACK.at[c]
+    PACK[c] = jnp.zeros(PACK.shape[1:], F32)
+    vectors_in = (ln1_gain_in, ln1_bias_in, ln2_gain_in, ln2_bias_in, out_bias_in, proj_bias_in, fc_bias_in)
+    for number, vector in enumerate(vectors_in):
+        PACK[c, number : number + 1, 0 : vector.shape[0]] = vector[...].astype(F32).reshape(1, -1)
+    PACK[c, 7:8, 0:doc_count] = doc_in[...].astype(F32)
+    for number in range(2):
+        PACK[c, 7:8, bias_first[number] : bias_first[number] + R] = qv_bias_in[number : number + 1, :].astype(F32)
     push(x_in, XG.at[zz, c], r_x_z, zdev)
     push(x_in, XG.at[zz, c], r_x_core, core)
-    push(pack_in, PACK.at[c], r_pack, core)
+    push(pack, pack, r_pack, core)
     push(w3_in, WB.at[:, 1, pl.ds(0, R)], r_w_core, (dp, z, 0), second_core)
     push(w3_in.at[:, pl.ds(0, TAIL)], WB.at[:, c, pl.ds(R, TAIL)], r_w_tail + c, (dp, jnp.maximum(z - 1, 0), 0), has_before)
     push(w3_in.at[:, pl.ds(0, TAIL)], WB.at[:, c, pl.ds(R, TAIL)], r_w_tail + c, (dp, lax.rem(z + 1, 4), 1), has_before)
-    push(pack_in, PACKF, r_packf, (dp, z2, 1), first_core)
+    push(pack, PACKF, r_packf, (dp, z2, 1), first_core)
+    push(pack, PACKN, r_packn, (dp, jnp.maximum(z - 1, 0), 0), has_before & first_core)
+    push(pack, PACKN, r_packn, (dp, lax.rem(z + 1, 4), 1), has_before & first_core)
     l_x = local(x_in, XG.at[zz, c])
-    l_pack = local(pack_in, PACK.at[c])
     l_w = local(w3_in, WB.at[:, 0, pl.ds(0, R)], first_core)
-    push(
-        fc_in.at[quarter_rows(jnp.minimum(dp, 1))], FB.at[c, my_quarter], r_f_z + c, (dp, z2, 1), dp < 2
-    )
-    push(
-        proj_in.at[quarter_rows(jnp.maximum(dp - 2, 0))],
-        FB.at[c, my_quarter],
-        r_f_z + c,
-        (dp, z2, 1),
-        dp >= 2,
-    )
-    for step in (1, 3, 2):
-        target = (dp, lax.rem(z + step, 4), c)
-        push(ow_in.at[ow_piece(0, dp)], OWB.at[c, ow_piece(z, dp)], r_o_z + z, target)
-        push(ow_in.at[ow_odd(0)], OWB.at[c, ow_odd(z)], r_o_z0 + z, target)
     push(fc_in, FB.at[1, pl.ds(0, H)], r_f_core, (dp, z, 0), second_core)
     push(proj_in, FB.at[1, pl.ds(H, H)], r_f_core + 1, (dp, z, 0), second_core)
     push(ow_in, OWB.at[c, block(z)], r_o_core, core)
@@ -613,21 +618,14 @@
     l_p = local(proj_in, FB.at[0, pl.ds(H, H)], first_core)
     l_o = local(ow_in, OWB.at[c, block(z)])
 
-    KD = N1.shape[2]
-    pad_rows = KD - H
-    ones_row = (lax.broadcasted_iota(jnp.int32, (pad_rows, T), 0) == 0).astype(BF)
-    for t in range(2):
-        for h in range(2):
-            N1[t, h, H:, :] = ones_row
     VGC[...] = jnp.zeros_like(VGC)
     GQKV[...] = jnp.zeros_like(GQKV)
 
     def clear_tail():
-        WB[:, :, R:, :] = jnp.zeros((3, 2, TAIL, HP), BF)
+        WB[:, :, R:, :] = jnp.zeros((3, 2, TAIL, H), BF)
 
     pl.when(j == 3)(clear_tail)
 
-    done(l_pack)
     arrived(PACK.at[oc], r_pack)
     lengths = PACK[pair, 7:8, 0:LANES]
     place_c = lax.broadcasted_iota(jnp.int32, (S, LANES), 0).astype(F32)
@@ -695,6 +693,20 @@
         )
     arrived(XG.at[1 - zz, c], r_x_z)
     e_xf = push(XG.at[1 - zz, c], XG.at[1 - zz, c], r_x_fwd, core)
+    for step in (1, 3, 2):
+        target = (dp, lax.rem(z + step, 4), c)
+        push(ow_in.at[ow_piece(0, dp)], OWB.at[c, ow_piece(z, dp)], r_o_z + z, target)
+        push(ow_in.at[ow_odd(0)], OWB.at[c, ow_odd(z)], r_o_z0 + z, target)
+    push(
+        fc_in.at[quarter_rows(jnp.minimum(dp, 1))], FB.at[c, my_quarter], r_f_z + c, (dp, z2, 1), dp < 2
+    )
+    push(
+        proj_in.at[quarter_rows(jnp.maximum(dp - 2, 0))],
+        FB.at[c, my_quarter],
+        r_f_z + c,
+        (dp, z2, 1),
+        dp >= 2,
+    )
 
     arrived(XG.at[1 - zz, oc], r_x_fwd)
     first_norm(1 - zz)
@@ -706,32 +718,35 @@
     for h in range(2):
         arrived(WB.at[:, h, pl.ds(R, TAIL)], r_w_tail + h, j < 3)
 
+    arrived(PACKF, r_packf, second_core)
+    arrived(PACKN, r_packn, j < 3)
+
+    def bias_columns(source, rows, count):
+        turned = source.T
+        for m, first in ((0, bias_first[0]), (2, bias_first[1])):
+            QB[rows : rows + count, m : m + 1] = turned[first : first + count, 7:8]
+
+    QB[...] = jnp.zeros_like(QB)
+    pl.when(first_core)(lambda: bias_columns(PACK[0], 0, R))
+    pl.when(second_core)(lambda: bias_columns(PACKF[...], 0, R))
+    pl.when(j < 3)(lambda: bias_columns(PACKN[...], R, TAIL))
+
     for t in range(2):
         for m in range(3):
-            mixed = dot_nn(WB[m, 0, :, 0:KD], N1[t, 0]) + dot_nn(WB[m, 1, :, 0:KD], N1[t, 1])
+            mixed = dot_nn(WB[m, 0], N1[t, 0]) + dot_nn(WB[m, 1], N1[t, 1])
+            if m != 1:
+                mixed = mixed + QB[:, m : m + 1]
             low = mixed.astype(BF)
             if m == 0:
                 low = low * jnp.asarray(score_scale, BF)
             QKV[m, :, t * T : (t + 1) * T] = low
 
-    for h in range(2):
-        arrived(FB.at[h, my_quarter], r_f_z + h, second_core)
-    ff_entries = []
-    for peer in peers:
-        ff_entries.append(
-            push(FB.at[:, my_quarter], FB.at[:, my_quarter], r_f_xy + dp, (peer, z, 1), second_core)
-        )
     for step in (1, 3, 2):
         there = lax.rem(z + step, 4)
         arrived(OWB.at[c, ow_piece(there, dp)], r_o_z + there)
         for peer in peers:
             rows = ow_piece(there, dp)
             push(OWB.at[c, rows], OWB.at[c, rows], r_o_xy + (4 * dp + there), (peer, z, c))
-    r_c_core, r_c_z, r_c_fwd = recvs.take(), recvs.take(), recvs.take()
-    push(cot_in, CG.at[zz, c], r_c_z, zdev)
-    push(cot_in, CG.at[zz, c], r_c_core, core)
-    l_c = local(cot_in, CG.at[zz, c])
-
     r_a_z, r_a_core, r_a_fwd = recvs.take(5), recvs.take(5), recvs.take(5)
     s_a_z, s_a_core, s_a_fwd = sends.take(5), sends.take(5), sends.take(5)
     first_slot = jnp.where(j == 0, 0, 1)
@@ -746,7 +761,20 @@
         rows = head_rows(owner, slot)
         return remote(ATT.at[rows], ATT.at[rows], s_base + slot, r_base + slot, dev)
 
+    s_f_xy = sends.take(3)
+
+    def ff_copy(number):
+        part = FB.at[:, my_quarter]
+        return remote(part, part, s_f_xy + number, r_f_xy + dp, (peers[number], z, 1))
+
     def attend(slot, carry):
+        @pl.when((slot == 4) & second_core)
+        def _():
+            for h in range(2):
+                arrived(FB.at[h, my_quarter], r_f_z + h)
+            for number in range(3):
+                ff_copy(number).start()
+
         rows = slot_rows(slot)
         out_rows = head_rows(j, slot)
         queries = QKV[0, rows, :]
@@ -770,8 +798,11 @@
 
     lax.fori_loop(first_slot, 5, attend, 0)
 
-    arrived(CG.at[1 - zz, c], r_c_z)
-    push(CG.at[1 - zz, c], CG.at[1 - zz, c], r_c_fwd, core)
+    r_c_core, r_c_z, r_c_fwd = recvs.take(), recvs.take(), recvs.take()
+    push(cot_in, CG.at[zz, c], r_c_z, zdev)
+    push(cot_in, CG.at[zz, c], r_c_core, core)
+    l_c = local(cot_in, CG.at[zz, c])
+
     for step in (1, 3, 2):
         there = lax.rem(z + step, 4)
         arrived(OWB.at[c, ow_odd(there)], r_o_z0 + there)
@@ -826,8 +857,6 @@
         arrived(FB.at[1, pl.ds(number * H, H)], r_f_core + number, first_core)
     for number in range(4):
         arrived(FB.at[:, quarter_rows(number)], r_f_xy + number, second_core & (dp != number))
-    arrived(PACKF, r_packf, second_core)
-
     @pl.when(first_core)
     def _():
         COLS[:, 6:7] = PACK[0].T[0:FW, 6:7]
@@ -836,6 +865,8 @@
     def _():
         COLS[:, 6:7] = PACKF[...].T[0:FW, 6:7]
 
+    arrived(CG.at[1 - zz, c], r_c_z)
+    push(CG.at[1 - zz, c], CG.at[1 - zz, c], r_c_fwd, core)
     done(l_c)
     arrived(CG.at[zz, oc], r_c_core)
     arrived(CG.at[1 - zz, oc], r_c_fwd)
@@ -874,8 +905,8 @@
 
     lax.fori_loop(0, n_tiles, feed, 0)
 
-    for entry in ff_entries:
-        sent(entry)
+    for number in range(3):
+        when(second_core, ff_copy(number).wait_send)
     r_f1, r_f2 = recvs.take(4), recvs.take(2)
     f1_entries = []
 
@@ -1072,9 +1103,13 @@
     lax.fori_loop(first_slot, 5, attend_back, 0)
 
     for m in range(3):
+        if m != 1:
+            bias_sum = jnp.sum(GQKV[m].astype(F32), axis=1, keepdims=True)
         for h in range(2):
             total = dot_nt(GQKV[m, :, 0:T], N1[0, h]) + dot_nt(GQKV[m, :, T:S], N1[1, h])
-            DQ[m, h, :, 0:KD] = total.astype(BF)
+            DQ[m, h, :, 0:H] = total.astype(BF)
+            if m != 1:
+                DQ[m, h, :, H : H + 1] = bias_sum.astype(BF)
         q1_push(0, m, m // 2, xdev, xb != m % 2)
         q1_push(1, m, 2 + m % 2, ydev, yb != m // 2)
 
@@ -1091,9 +1126,9 @@
 
     def back_rows(half, tile):
         all_cols = pl.ds(pl.multiple_of(tile * W, W), W)
-        total = dot_tn(WB[0, half, :, 0:H], GQKV[0, :, all_cols])
+        total = dot_tn(WB[0, half], GQKV[0, :, all_cols])
         for m in range(1, 3):
-            total = total + dot_tn(WB[m, half, :, 0:H], GQKV[m, :, all_cols])
+            total = total + dot_tn(WB[m, half], GQKV[m, :, all_cols])
         return total
 
     def first_part(tile, carry):
@@ -1299,13 +1334,14 @@
     GQ,
     FST,
     QST,
+    OB,
     SEM,
 ):
     R, H = ow_o.shape
     count = GF.shape[0] // R
     whole = [
-        pltpu.make_async_copy(out_in, out_o, SEM.at[0]),
-        pltpu.make_async_copy(ing_in, ing_o, SEM.at[1]),
+        pltpu.make_async_copy(out_in, OB.at[0], SEM.at[0]),
+        pltpu.make_async_copy(ing_in, OB.at[1], SEM.at[1]),
     ]
     place = 2
     loads_q, loads_f = [], []
@@ -1334,13 +1370,18 @@
         dst = qkv_o.at[m] if m < 3 else ow_o
         stores.append(pltpu.make_async_copy(QST.at[m], dst, SEM.at[place + m]))
         stores[-1].start()
+    place += 4
+    for number, dst in enumerate((out_o, ing_o)):
+        whole[number].wait()
+        stores.append(pltpu.make_async_copy(OB.at[number], dst, SEM.at[place + number]))
+        stores[-1].start()
     first = H // LANES * LANES
     for number, m in enumerate((0, 2)):
         turned = GQ[m, :, first : first + LANES].astype(F32).T
         qvb_o[number : number + 1, :] = turned[H - first : H - first + 1, :]
     for number, v in enumerate((v0, v1, v2, v3, v4, v5, v6)):
         v[...] = vec_in[number, 0 : v.shape[0]]
-    for copy in stores + whole:
+    for copy in stores:
         copy.wait()
 
 
@@ -1368,23 +1409,8 @@
     HP = (H // LANES + 1) * LANES
     EXT = 5 * HEAD_DIM
     NT = S // KEY_TILE
-    doc_count = doc_lengths.shape[1]
-    first_core = lax.axis_index("col") == 0
-    low_bias = jnp.where(first_core, qv_bias, jnp.zeros_like(qv_bias))
-    bias_three = jnp.stack([low_bias[0], jnp.zeros_like(low_bias[0]), low_bias[1]])
-    w3 = jnp.concatenate(
-        [
-            jnp.transpose(qkv_weight, (1, 2, 0)),
-            bias_three[:, :, None],
-            jnp.zeros((3, R, HP - H - 1), BF),
-        ],
-        axis=2,
-    )
-    rows = [ln1_gain, ln1_bias, ln2_gain, ln2_bias, out_bias, proj_bias, fc_bias, doc_lengths[0]]
     wide = (FW // LANES + 1) * LANES
-    pack = jnp.concatenate(
-        [jnp.pad(row.astype(F32)[None], ((0, 0), (0, wide - row.shape[0]))) for row in rows], axis=0
-    )
+    w3 = jnp.transpose(qkv_weight, (1, 2, 0))
     shape = jax.ShapeDtypeStruct
     anywhere = pl.BlockSpec(memory_space=pl.ANY)
     outs = [
@@ -1403,12 +1429,14 @@
     scratch = [
         vmem((2, 2, H, T), BF),
         vmem((2, 2, H, T), BF),
-        vmem((2, 2, H + 16, T), BF),
-        vmem((3, 2, EXT, HP), BF),
+        vmem((2, 2, H, T), BF),
+        vmem((3, 2, EXT, H), BF),
+        vmem((EXT, LANES), F32),
         vmem((2, D, H), BF),
         vmem((2, 2 * H, FW), BF),
         vmem((FW, LANES), F32),
         vmem((2, 8, wide), F32),
+        vmem((8, wide), F32),
         vmem((8, wide), F32),
         vmem((mask_rows, KEY_TILE), F32),
         vmem((3, EXT, S), BF),
@@ -1450,15 +1478,31 @@
         pltpu.SemaphoreType.DMA((LOCAL_COUNT,)),
     ]
     out_rows, in_rows, gf, gq, vectors = pl.pallas_call(
-        partial(layer_kernel, doc_count=doc_count),
+        layer_kernel,
         out_shape=outs,
-        in_specs=[anywhere] * 7,
+        in_specs=[anywhere] * 6 + [pl.BlockSpec(memory_space=vmem)] * 9,
         out_specs=[anywhere] * len(outs),
         scratch_shapes=scratch,
         compiler_params=pltpu.CompilerParams(
             collective_id=0, has_side_effects=True, vmem_limit_bytes=VMEM_LIMIT
         ),
-    )(tokens, cotangent, w3, out_weight, fc_weight, proj_weight, pack)[:5]
+    )(
+        tokens,
+        cotangent,
+        w3,
+        out_weight,
+        fc_weight,
+        proj_weight,
+        ln1_gain,
+        ln1_bias,
+        ln2_gain,
+        ln2_bias,
+        out_bias,
+        proj_bias,
+        fc_bias,
+        qv_bias,
+        doc_lengths,
+    )[:5]
     in_vmem = pl.BlockSpec(memory_space=vmem)
     finals = pl.pallas_call(
         finish_kernel,
@@ -1480,9 +1524,10 @@
             vmem((4, R, HP), BF),
             vmem((D, FW), F32),
             vmem((4, R, H), F32),
+            vmem((2, H, T), BF),
             pltpu.SemaphoreType.DMA((32,)),
         ],
-        compiler_params=pltpu.CompilerParams(vmem_limit_bytes=32_000_000),
+        compiler_params=pltpu.CompilerParams(vmem_limit_bytes=VMEM_LIMIT),
     )(out_rows, in_rows, gf, gq, vectors)
     out_final, in_final, qkv_rows, bias_grad, ow_grad, fc_grad, proj_grad = finals[:7]
     ln1_gain_g, ln1_bias_g, ln2_gain_g, ln2_bias_g, out_bias_g, proj_bias_g, fc_bias_g = finals[7:]

time: 282 us -> 259 us (0.918)
  local copies, waits for them, and re-layouts: 11.8 us -> 0 us
  Pallas kernels: 264 us -> 258 us
  other arithmetic: 3.92 us -> 0 us
    pallas_call x1, Pallas kernels: 259 us -> 252 us  [fast_body(): pl.pallas_call(layer_kernel, out_shape=outs, in_specs=[anywhere] * 6 + [p...]
    unnamed x10 -> x0, local copies, waits for them, and re-layouts: 5.92 us -> none
    broadcast_in_dim x9 -> x0, local copies, waits for them, and re-layouts: 5.03 us -> none  [the longest x7 4.82 us: fast_body(): row.astype(F32)[None]]
where the time goes in v3:
time: 259 us
  Pallas kernels  258 us (100%)
    pallas_call x1, Pallas kernels, fast_body(): pl.pallas_call(layer_kernel, out_shape=outs, in_specs=[anywhere] * 6 + [p...  252 us
    pallas_call x1, Pallas kernels, fast_body(): pl.pallas_call(finish_kernel, out_shape=[shape((H, T), BF), shape((H, T),...  6.3 us

profile of v3, /device:TPU:0, one launch (start us, length us, event | category | flops | bytes accessed | tf_op | source)
XLA Modules:
  0.0 258.7 jit_solution(10338258758851393928)
XLA Ops:
  0.7 251.5 %shard_map.254 = (bf16[544,512]{1,0:T(8,128)(2,1)}, bf16[544,512]{1,0:T(8,128)(2,1)}, bf16[1088,1088]{1,0:T(8,128)(2,1)}, bf16[4,272,640]{2,1,0:T(8,128)(2,1)}, ...) custom-call(bf16[544,512]{1,0:T(8,128)(2,1)} %x_in.1, ...), custom_call_target="tpu_custom_call" | custom-call | tf_op jit(solution)/shard_map/pallas_call | solution.py:1480
  252.2 6.3 %shard_map.255 = (bf16[544,512]{1,0:T(8,128)(2,1)}, bf16[544,512]{1,0:T(8,128)(2,1)}, f32[3,272,544]{2,1,0:T(8,128)}, f32[2,272]{1,0:T(2,128)}, f32[272,544]{1,0...) custom-call(bf16[544,512]{1,0:T(8,128)(2,1)} %get-tuple-element.33.o, ...), custom_call_target="tpu_custom_call" | custom-call | tf_op jit(solution)/shard_map/pallas_call | solution.py:1507
